TPU v7x, 32 devices: a whole 2x2x4 slice. The times are simulated.
32 devices in a mesh: grp: 2 (over core), head: 4 (over y, x), seq: 4 (over z).
Axes of the slice: x: 2, y: 2, z: 4, core: 2. Of those that a mesh axis runs over, the one named last changes fastest.
Arguments:
- seq_in: bfloat16 [4096, 4096], P('seq', 'head'), may hold values from -36 to 36
- w_proj: bfloat16 [2, 3, 4096, 4096], P('grp', None, None, 'head')
- w_out: bfloat16 [2, 4096, 4096], P('grp', 'head'), may hold values from -0.09375 to 0.09375
- filters: float32 [4096, 4096], P(('head', 'seq'))
Outputs:
- paired: bfloat16 [2, 4096, 4096], P('grp', 'seq', 'head')
- grad_filters: float32 [4096, 4096], P(('head', 'seq'), 'grp')
All inputs are finite; a program needn't handle non-finite values.
Results may differ from a plain program's by a relative error of at most 0.015.
Values may be sent and summed in bfloat16 or wider, within the bound.
A program may use at most 256 MiB of HBM per device.

v0:
```python
import math

import jax
import jax.numpy as jnp
from jax import lax
from jax.sharding import PartitionSpec as P

HD = 128


exact_math = lax.Precision.HIGHEST
very_low = -1e30


def passed_along(value, axis, by):
    devices = lax.axis_size(axis)
    pairs = [(i, i + by) for i in range(devices) if 0 <= i + by < devices]
    return lax.ppermute(value, axis, pairs)


def dft_tables(length):
    total_len = 2 * length
    outer_len = total_len // 128
    half_len = outer_len // 2
    outer_idx = jnp.arange(outer_len, dtype=jnp.int32)
    inner_idx = jnp.arange(128, dtype=jnp.int32)
    angle_outer = (
        -2.0
        * math.pi
        / outer_len
        * (outer_idx[:, None] * outer_idx[None, :] % outer_len).astype(jnp.float32)
    )
    angle_inner = (
        -2.0 * math.pi / 128 * (inner_idx[:, None] * inner_idx[None, :] % 128).astype(jnp.float32)
    )
    angle_twist = (
        -2.0
        * math.pi
        / total_len
        * (outer_idx[:, None] * inner_idx[None, :] % total_len).astype(jnp.float32)
    )
    cos_outer = jnp.cos(angle_outer)
    sin_outer = jnp.sin(angle_outer)
    cos_inner = jnp.cos(angle_inner)
    sin_inner = jnp.sin(angle_inner)
    forward_inner = jnp.concatenate(
        [
            jnp.concatenate([cos_inner, sin_inner], axis=1),
            jnp.concatenate([-sin_inner, cos_inner], axis=1),
        ],
        axis=0,
    )
    inverse_inner = jnp.concatenate(
        [
            jnp.concatenate([cos_inner, -sin_inner], axis=1),
            jnp.concatenate([sin_inner, cos_inner], axis=1),
        ],
        axis=0,
    )
    inverse_outer = jnp.concatenate([cos_outer[:half_len], sin_outer[:half_len]], axis=1)
    return (
        cos_outer[:, :half_len],
        sin_outer[:, :half_len],
        jnp.cos(angle_twist),
        jnp.sin(angle_twist),
        forward_inner,
        inverse_inner,
        inverse_outer,
    )


def forward_dft(field, tables):
    cos_first, sin_first, cos_twist, sin_twist, forward_inner, inverse_inner, inverse_outer = tables
    channels = field.shape[0]
    blocks = field.reshape(channels, cos_first.shape[1], 128)
    real_a = jnp.einsum("kn,cnm->ckm", cos_first, blocks, precision=exact_math)
    imag_a = jnp.einsum("kn,cnm->ckm", sin_first, blocks, precision=exact_math)
    real_b = real_a * cos_twist - imag_a * sin_twist
    imag_b = real_a * sin_twist + imag_a * cos_twist
    spectrum = jnp.einsum(
        "ckm,mj->ckj",
        jnp.concatenate([real_b, imag_b], axis=2),
        forward_inner,
        precision=exact_math,
    )
    return (spectrum[:, :, :128], spectrum[:, :, 128:])


def inverse_dft(real_x, imag_x, tables):
    cos_first, sin_first, cos_twist, sin_twist, forward_inner, inverse_inner, inverse_outer = tables
    mixed_b = jnp.einsum(
        "ckm,mj->ckj",
        jnp.concatenate([real_x, imag_x], axis=2),
        inverse_inner,
        precision=exact_math,
    )
    real_b = mixed_b[:, :, :128]
    imag_b = mixed_b[:, :, 128:]
    real_c = real_b * cos_twist + imag_b * sin_twist
    imag_c = imag_b * cos_twist - real_b * sin_twist
    field = jnp.einsum(
        "nk,ckm->cnm",
        inverse_outer,
        jnp.concatenate([real_c, imag_c], axis=1),
        precision=exact_math,
    )
    scale_back = 1.0 / (cos_twist.shape[0] * 128)
    return field.reshape(field.shape[0], -1) * scale_back


def student_forward(operands, tables, tap_scale):
    fields, filters = operands
    value_s = fields[0].astype(jnp.float32)
    gate_in = fields[1].astype(jnp.float32)
    gate_out = fields[2].astype(jnp.float32)
    carried = gate_in * value_s
    real_u, imag_u = forward_dft(carried, tables)
    real_h, imag_h = forward_dft(filters * tap_scale, tables)
    conv = inverse_dft(real_u * real_h - imag_u * imag_h, real_u * imag_h + imag_u * real_h, tables)
    gated = (gate_out * conv).astype(jnp.bfloat16)
    return (gated, conv, (real_u, imag_u, real_h, imag_h))


def student_backward(operands, tables, tap_scale):
    fields, d_gated, conv, spectra = operands
    value_s = fields[0].astype(jnp.float32)
    gate_in = fields[1].astype(jnp.float32)
    gate_out = fields[2].astype(jnp.float32)
    real_u, imag_u, real_h, imag_h = spectra
    grad_gated = d_gated.astype(jnp.float32)
    d_conv = gate_out * grad_gated
    d_gate_out = (conv * grad_gated).astype(jnp.bfloat16)
    real_d, imag_d = forward_dft(d_conv, tables)
    d_carried = inverse_dft(
        real_h * real_d + imag_h * imag_d, real_h * imag_d - imag_h * real_d, tables
    )
    d_taps = inverse_dft(
        real_u * real_d + imag_u * imag_d, real_u * imag_d - imag_u * real_d, tables
    )
    d_gate_in = (d_carried * value_s).astype(jnp.bfloat16)
    d_value = (d_carried * gate_in).astype(jnp.bfloat16)
    return (jnp.stack([d_value, d_gate_in, d_gate_out]), d_taps * tap_scale)


def body(seq_in, w_proj, w_out, filters):
    teacher = lax.axis_index("grp") == 0
    row_count = seq_in.shape[0]
    weights_in = w_proj[0]
    weights_out = w_out[0]
    col_count = weights_in.shape[2]
    seq_count = lax.axis_size("seq")
    chan_count = col_count // seq_count
    length = row_count * seq_count
    outer_len = 2 * length // 128
    tap_scale = length ** (-0.5)
    block = weights_in
    projected = lax.dot_general(
        block,
        lax.all_gather(seq_in, "head", axis=1, tiled=True),
        (((1,), (1,)), ((), ())),
        preferred_element_type=jnp.float32,
    ).astype(jnp.bfloat16)
    head_count = col_count // HD
    parts = projected.reshape(3, head_count, HD, row_count)
    query = parts[0]
    first_row = lax.axis_index("seq") * row_count
    query_pos = first_row + jnp.arange(row_count, dtype=jnp.int32)
    factor = HD ** (-0.5)
    start_state = (
        jnp.full((head_count, row_count), very_low, jnp.float32),
        jnp.zeros((head_count, row_count), jnp.float32),
        jnp.zeros((head_count, HD, row_count), jnp.float32),
    )
    key_part = lax.all_gather(parts[1], "seq", axis=2, tiled=True)
    value_part = lax.all_gather(parts[2], "seq", axis=2, tiled=True)
    part_len = key_part.shape[2]
    step_len = math.gcd(part_len, 512)

    def one_block(block_no, status):
        offset = block_no * step_len
        key_blk = lax.dynamic_slice_in_dim(key_part, offset, step_len, 2)
        value_blk = lax.dynamic_slice_in_dim(value_part, offset, step_len, 2)
        key_pos = offset + jnp.arange(step_len, dtype=jnp.int32)

        def attend(inner):
            running_max, running_sum, running_acc = inner
            scores = (
                jnp.einsum("hdi,hdj->hij", query, key_blk, preferred_element_type=jnp.float32)
                * factor
            )
            scores = jnp.where(key_pos[None, None, :] <= query_pos[None, :, None], scores, -jnp.inf)
            new_max = jnp.maximum(running_max, jnp.max(scores, axis=2))
            expos = jnp.exp(scores - new_max[:, :, None])
            fading = jnp.exp(running_max - new_max)
            new_sum = running_sum * fading + jnp.sum(expos, axis=2)
            product = jnp.einsum(
                "hij,hdj->hdi",
                expos.astype(jnp.bfloat16),
                value_blk,
                preferred_element_type=jnp.float32,
            )
            return (new_max, new_sum, running_acc * fading[:, None, :] + product)

        def keep(inner):
            return inner

        return lax.cond(teacher, attend, keep, status)

    final_max, final_sum, final_acc = lax.fori_loop(0, part_len // step_len, one_block, start_state)
    attended = (
        (final_acc / jnp.where(teacher, final_sum, 1.0)[:, None, :])
        .reshape(col_count, row_count)
        .astype(jnp.bfloat16)
    )
    spread = lax.all_to_all(
        projected.reshape(3, seq_count, chan_count, row_count),
        "seq",
        split_axis=1,
        concat_axis=3,
        tiled=True,
    )
    fields_c = spread.reshape(3, chan_count, length)
    tables = dft_tables(length)

    def run_student(operands):
        return student_forward(operands, tables, tap_scale)

    def spare_student(operands):
        zero_spec = jnp.zeros((chan_count, outer_len, 128), jnp.float32)
        return (
            jnp.zeros((chan_count, length), jnp.bfloat16),
            jnp.zeros((chan_count, length), jnp.float32),
            (zero_spec, zero_spec, zero_spec, zero_spec),
        )

    gated, conv, spectra = lax.cond(teacher, spare_student, run_student, (fields_c, filters))
    returned = lax.all_to_all(gated, "seq", split_axis=1, concat_axis=0, tiled=True)
    mixed = jnp.where(teacher, attended, returned)
    y_own = lax.psum_scatter(
        lax.dot_general(
            weights_out, mixed, (((0,), (0,)), ((), ())), preferred_element_type=jnp.float32
        ).astype(jnp.bfloat16),
        "head",
        scatter_dimension=0,
        tiled=True,
    )
    target = passed_along(y_own, "grp", 1)
    diff = (y_own.astype(jnp.float32) - target.astype(jnp.float32)).astype(jnp.bfloat16)
    portion = lax.all_gather(diff, "head", axis=0, tiled=True)
    block = weights_out

    def keep_sum(current):
        return current

    def grow_sum(current):
        return jnp.dot(block, portion, preferred_element_type=jnp.float32)

    d_gated = lax.cond(
        teacher, keep_sum, grow_sum, jnp.zeros((col_count, row_count), jnp.float32)
    ).astype(jnp.bfloat16)
    d_spread = lax.all_to_all(
        d_gated.reshape(seq_count, chan_count, row_count),
        "seq",
        split_axis=0,
        concat_axis=2,
        tiled=True,
    ).reshape(chan_count, length)

    def run_backward(operands):
        return student_backward(operands, tables, tap_scale)

    def spare_backward(operands):
        return (
            jnp.zeros((3, chan_count, length), jnp.bfloat16),
            jnp.zeros((chan_count, length), jnp.float32),
        )

    d_fields, d_taps = lax.cond(
        teacher, spare_backward, run_backward, (fields_c, d_spread, conv, spectra)
    )
    d_rows = lax.all_to_all(d_fields, "seq", split_axis=2, concat_axis=1, tiled=True)

    def skip_grad(operand):
        return jnp.zeros((lax.axis_size("head") * col_count, row_count), jnp.float32)

    def make_grad(operand):
        return lax.dot_general(
            weights_in, operand, (((0, 2), (0, 1)), ((), ())), preferred_element_type=jnp.float32
        )

    d_input = lax.psum_scatter(
        lax.cond(teacher, skip_grad, make_grad, d_rows).astype(jnp.bfloat16),
        "head",
        scatter_dimension=0,
        tiled=True,
    )
    paired = jnp.where(teacher, y_own.T, d_input.T)[None]
    half_len = length // 2
    lower_taps = passed_along(d_taps[:, :half_len].astype(jnp.bfloat16), "grp", -1).astype(
        jnp.float32
    )
    grad_filters = jnp.where(teacher, lower_taps, d_taps[:, half_len:])
    return (paired, grad_filters)


def solution(mesh):
    return jax.shard_map(
        body,
        mesh=mesh,
        in_specs=(
            P("seq", "head"),
            P("grp", None, None, "head"),
            P("grp", "head", None),
            P(("head", "seq"), None),
        ),
        out_specs=(P("grp", "seq", "head"), P(("head", "seq"), "grp")),
        check_vma=False,
    )
```

profile of v0, /device:TPU:1, one launch (start us, length us, event | category | flops | bytes accessed | tf_op | source)
XLA Modules:
  0.0 1662.7 jit_solution(16666733938304703578)
XLA Ops:
  7.9 91.6 %all-gather.5.cloned.1.call-done = bf16[1024,4096]{1,0:T(8,128)(2,1)} async-done(((bf16[1024,1024]{1,0:T(8,128)(2,1)}), bf16[1024,4096]{1,0:T(8,128)(2,1)}) %all-gather.5.cloned.1.call-update) | async-done | bytes 8388624 | tf_op jit(solution)/shard_map/all_gather | solution.py:159
  99.6 32.1 %fusion.84 = bf16[3,1024,1024]{2,1,0:T(8,128)(2,1)S(1)} fusion(bf16[1024,4096]{1,0:T(8,128)(2,1)} %all-gather.5.cloned.1.call-done, bf16[1,3,4096,1024]{3,2,1,0:T(8,128)(2,1)} %param.17), kind=kOutput, calls=%fused_computation.131 | convolution fusion | flops 25772949504 | bytes 39845888 | tf_op jit(solution)/shard_map/dot_general | solution.py:157
  157.2 264.1 %all-to-all-done = bf16[3,4,256,1024]{3,2,0,1:T(8,128)(2,1)} async-done(((bf16[3,4,256,1024]{3,2,0,1:T(8,128)(2,1)}), bf16[3,4,256,1024]{3,2,0,1:T(8,128)(2,1)}, u32[]{:S(2)}, u32[]{:S(2)}) %all-to-all-start) | async-done | bytes 6291488 | tf_op jit(solution)/shard_map/all_to_all | solution.py:215
  421.3 8.8 copy.99
  430.0 271.6 %conditional.5 = (bf16[256,4096]{1,0:T(8,128)(2,1)S(1)}, f32[256,4096]{1,0:T(8,128)}, f32[256,64,128]{0,2,1:T(8,128)}, f32[256,64,128]{0,2,1:T(8,128)}, f32[256,...) conditional(s32[]{:T(128)} %convert_element_type.198, (bf16[3,256,4096]{1,2,0:T(8,128)(2,1)}, f32[64,32]{1,0:T(8,128)}, ...), branch_computations={%region_6.7_spmd, %region_7.8_spmd} | conditional | flops 43562041344 | bytes 533905472 | solution.py:236
  435.9 8.7 copy.100
  448.4 7.8 fusion.46
  456.2 12.6 fusion.32
  468.8 9.8 pad_maximum_fusion
  478.6 42.4 %fusion.28 = f32[256,64,256]{0,2,1:T(8,128)} fusion(f32[256,64,256]{2,1,0:T(8,128)} %pad_maximum_fusion, f32[256,256]{1,0:T(8,128)} %get-tuple-element.638), kind=kOutput, calls=%fused_computation.35 | convolution fusion | flops 12884901888 | bytes 33816576 | tf_op jit(solution)/shard_map/cond/branch_0_fun/ckm,mj->ckj/dot_general | solution.py:80
  520.9 7.8 fusion.42
  528.8 12.0 fusion.30
  540.8 9.6 pad_maximum_fusion.1
  550.4 32.7 %fusion.26 = f32[256,64,256]{0,2,1:T(8,128)} fusion(f32[256,64,256]{2,1,0:T(8,128)} %pad_maximum_fusion.1, f32[256,256]{1,0:T(8,128)} %get-tuple-element.638), kind=kOutput, calls=%fused_computation.33 | convolution fusion | flops 12884901888 | bytes 33816576 | tf_op jit(solution)/shard_map/cond/branch_0_fun/ckm,mj->ckj/dot_general | solution.py:80
  583.2 25.2 %multiply_subtract_fusion.1 = (f32[256,64,128]{0,2,1:T(8,128)}, f32[256,64,128]{0,2,1:T(8,128)}, f32[256,64,128]{0,2,1:T(8,128)}, f32[256,64,128]{0,2,1:T(8,128)}, f32[256,64,128]{0,2,1:T(8,128)}) fusion(f32[256,64,256]{0,2,1:T(8,128)} %fusion.26, f32[256,64,256]{0,2,1:T(8,128)} %fusion.28), kind=kLoop, calls=%fused_computation.52 | loop fusion | flops 6291456 | bytes 75497472 | tf_op jit(solution)/shard_map/cond/branch_0_fun/sub | solution.py:119
  608.3 16.1 multiply_add_fusion.3
  624.4 33.8 %fusion.20 = f32[256,64,256]{2,0,1:T(8,128)} fusion(f32[256,64,128]{0,2,1:T(8,128)} %multiply_add_fusion.3, f32[256,64,128]{0,2,1:T(8,128)} %get-tuple-element.697, f32[256,256]{1,0:T(8,128)} %get-tuple-element.396), kind=kOutput, calls=%fused_computation.26 | convolution fusion | flops 12889096192 | bytes 33816576 | tf_op jit(solution)/shard_map/cond/branch_0_fun/ckm,mj->ckj/dot_general | solution.py:91
  658.2 8.7 multiply_add_fusion.2
  669.3 24.2 %broadcast_multiply_fusion = f32[256,128,32]{1,2,0:T(8,128)S(1)} fusion(f32[256,128,128]{2,0,1:T(8,128)S(1)} %pad_maximum_fusion.2, f32[32,128]{1,0:T(8,128)} %get-tuple-element.401), kind=kOutput, calls=%fused_computation.59 | convolution fusion | flops 1611661312 | bytes 20987904 | tf_op jit(solution)/shard_map/cond/branch_0_fun/nk,ckm->cnm/dot_general | solution.py:101
  693.5 7.9 fusion.34
  715.6 18.0 %all-to-all-done.1 = bf16[256,4,1024]{2,0,1:T(8,128)(2,1)} async-done(((bf16[256,4,1024]{2,0,1:T(8,128)(2,1)}), bf16[256,4,1024]{2,0,1:T(8,128)(2,1)}, u32[]{:S(2)}, u32[]{:S(2)}) %all-to-all-start.1) | async-done | bytes 2097184 | tf_op jit(solution)/shard_map/all_to_all | solution.py:237
  735.4 14.7 convert_bitcast_fusion.1
  750.2 206.0 %reduce-scatter.3.cloned.1.call-done = bf16[1024,1024]{0,1:T(8,128)(2,1)} async-done(((bf16[4096,1024]{0,1:T(8,128)(2,1)}), bf16[1024,1024]{0,1:T(8,128)(2,1)}) %reduce-scatter.3.cloned.1.call-update) | async-done | bytes 2097168 | tf_op jit(solution)/shard_map/reduce_scatter | solution.py:239
  966.4 87.3 %all-gather.11.cloned.1.call-done = bf16[4096,1024]{0,1:T(8,128)(2,1)} async-done(((bf16[1024,1024]{0,1:T(8,128)(2,1)}), bf16[4096,1024]{0,1:T(8,128)(2,1)}) %all-gather.11.cloned.1.call-update) | async-done | bytes 8388624 | tf_op jit(solution)/shard_map/all_gather | solution.py:249
  1053.7 13.7 conditional.6
  1053.7 13.7 fusion.117
  1073.1 36.4 %all-to-all-done.2 = bf16[4,256,1024]{2,1,0:T(8,128)(2,1)S(1)} async-done(((bf16[4,256,1024]{2,1,0:T(8,128)(2,1)}), bf16[4,256,1024]{2,1,0:T(8,128)(2,1)S(1)}, u32[]{:S(2)}, u32[]{:S(2)}) %all-to-all-start.2) | async-done | bytes 2097184 | tf_op jit(solution)/shard_map/all_to_all | solution.py:261
  1109.4 287.3 %conditional.7 = (bf16[3,256,4096]{2,1,0:T(8,128)(2,1)}, f32[256,4096]{1,0:T(8,128)}) conditional(s32[]{:T(128)} %convert_element_type.198, (bf16[3,256,4096]{1,2,0:T(8,128)(2,1)}, bf16[1,256,4,1024]{3,1,2,0:T(8,128)(2,1)S(1)}, f32[64,32]{1,0:T(8,128)}, f32[64,128]{1,0:T(8,128)}, f32[64,128]{1,0:T(8,128)}, /*index=5*/f32[64,128]{1,0:T(8,128)}, ...), branch_computations={%region_11.12_spmd, %region_12.13_spmd} | conditional | flops 43589304320 | bytes 594722944 | solution.py:278
  1127.1 8.6 copy.108
  1139.7 7.8 fusion.76
  1147.6 12.6 fusion.64
  1160.1 9.8 pad_maximum_fusion.3
  1169.9 32.7 %fusion.62 = f32[256,64,256]{0,2,1:T(8,128)} fusion(f32[256,64,256]{2,1,0:T(8,128)} %pad_maximum_fusion.3, f32[256,256]{1,0:T(8,128)} %get-tuple-element.662), kind=kOutput, calls=%fused_computation.88 | convolution fusion | flops 12884901888 | bytes 33816576 | tf_op jit(solution)/shard_map/cond/branch_0_fun/ckm,mj->ckj/dot_general | solution.py:80
  1202.7 29.3 %multiply_add_fusion.5 = (f32[256,64,128]{0,2,1:T(8,128)}, f32[256,64,128]{0,2,1:T(8,128)}, f32[256,64,128]{0,2,1:T(8,128)}, f32[256,64,128]{0,2,1:T(8,128)}) fusion(f32[256,64,128]{0,2,1:T(8,128)} %get-tuple-element.423, f32[256,64,128]{0,2,1:T(8,128)} %get-tuple-element.422, f32[256,64,256]{0,2,1:T(8,128)} %fusion.62, ...), kind=kLoop, calls=%fused_computation.99 | loop fusion | flops 25165824 | bytes 83886080 | tf_op jit(solution)/shard_map/cond/branch_0_fun/add | solution.py:138
  1231.9 33.6 %fusion.54 = f32[256,64,256]{2,0,1:T(8,128)} fusion(f32[256,64,128]{0,2,1:T(8,128)} %get-tuple-element.703, f32[256,64,128]{0,2,1:T(8,128)} %get-tuple-element.702, f32[256,256]{1,0:T(8,128)} %get-tuple-element.415), kind=kOutput, calls=%fused_computation.79 | convolution fusion | flops 12889096192 | bytes 33816576 | tf_op jit(solution)/shard_map/cond/branch_0_fun/ckm,mj->ckj/dot_general | solution.py:91
  1265.6 33.7 %fusion.50 = f32[256,64,256]{2,0,1:T(8,128)} fusion(f32[256,64,128]{0,2,1:T(8,128)} %get-tuple-element.708, f32[256,64,128]{0,2,1:T(8,128)} %get-tuple-element.709, f32[256,256]{1,0:T(8,128)} %get-tuple-element.415), kind=kOutput, calls=%fused_computation.74 | convolution fusion | flops 12889096192 | bytes 33816576 | tf_op jit(solution)/shard_map/cond/branch_0_fun/ckm,mj->ckj/dot_general | solution.py:91
  1299.3 19.9 %multiply_add_fusion.4 = (f32[256,64,128]{2,0,1:T(8,128)}, f32[256,64,128]{2,0,1:T(8,128)}, f32[256,64,128]{2,0,1:T(8,128)S(1)}, f32[256,64,128]{2,0,1:T(8,128)S(1)}) fusion(f32[256,64,256]{2,0,1:T(8,128)} %fusion.54, f32[64,128]{1,0:T(8,128)} %get-tuple-element.425, f32[64,128]{1,0:T(8,128)} %get-tuple-element.424, f32[64,128]{1,0:T(8,128)} %get-tuple-element.427, ...), kind=kLoop, calls=%fused_computation.97 | loop fusion | flops 25165824 | bytes 67371008 | tf_op jit(solution)/shard_map/cond/branch_0_fun/add | solution.py:99
  1319.2 7.0 pad_maximum_fusion.5
  1326.2 24.0 %broadcast_multiply_fusion.1 = f32[256,128,32]{1,2,0:T(8,128)S(1)} fusion(f32[256,128,128]{2,0,1:T(8,128)S(1)} %pad_maximum_fusion.5, f32[32,128]{1,0:T(8,128)} %get-tuple-element.420), kind=kOutput, calls=%fused_computation.113 | convolution fusion | flops 1611661312 | bytes 20987904 | tf_op jit(solution)/shard_map/cond/branch_0_fun/nk,ckm->cnm/dot_general | solution.py:101
  1358.5 25.2 %multiply_bitcast_fusion.2 = f32[256,32,128]{2,1,0:T(8,128)} fusion(f32[256,128,128]{2,0,1:T(8,128)S(1)} %pad_maximum_fusion.4, f32[32,128]{1,0:T(8,128)} %get-tuple-element.420), kind=kOutput, calls=%fused_computation.111 | convolution fusion | flops 1611661312 | bytes 20987904 | tf_op jit(solution)/shard_map/cond/branch_0_fun/nk,ckm->cnm/dot_general | solution.py:101
  1396.8 13.1 copy.113
  1415.5 93.4 %all-to-all-done.3 = bf16[3,256,4096]{1,0,2:T(4,128)(2,1)} async-done(((bf16[3,256,4096]{1,0,2:T(4,128)(2,1)}), bf16[3,256,4096]{1,0,2:T(4,128)(2,1)}, u32[]{:S(2)}, u32[]{:S(2)}) %all-to-all-start.3) | async-done | bytes 6291488 | tf_op jit(solution)/shard_map/all_to_all | solution.py:281
  1508.9 6.9 copy.114
  1515.9 41.2 %conditional.8 = (bf16[4096,1024]{1,0:T(8,128)(2,1)}) conditional(s32[]{:T(128)} %convert_element_type.198, (bf16[3,4,256,1024]{2,3,1,0:T(8,128)(2,1)}, bf16[3,4096,1024]{2,1,0:T(8,128)(2,1)}) %tuple.169, () %tuple.78), branch_computations={%region_13.14_spmd, %region_14.15_spmd} | conditional | flops 25769803776 | bytes 52428808 | solution.py:292
  1515.9 8.6 copy.115
  1524.5 32.5 %convolution_bitcast_fusion = bf16[4096,1024]{1,0:T(8,128)(2,1)} fusion(bf16[3,4096,1024]{2,1,0:T(8,128)(2,1)} %get-tuple-element.428, bf16[3,1024,1024]{2,1,0:T(8,128)(2,1)} %bitcast.214), kind=kOutput, calls=%fused_computation.125 | convolution fusion | flops 25769803776 | bytes 39845888 | tf_op jit(solution)/shard_map/cond/branch_0_fun/dot_general | solution.py:287
  1557.0 11.2 copy.116
  1577.1 75.3 %reduce-scatter.5.cloned.1.call-done = bf16[1024,1024]{0,1:T(8,128)(2,1)} async-done(((bf16[4096,1024]{0,1:T(8,128)(2,1)}), bf16[1024,1024]{0,1:T(8,128)(2,1)}) %reduce-scatter.5.cloned.1.call-update) | async-done | bytes 2097168 | tf_op jit(solution)/shard_map/reduce_scatter | solution.py:291
  (103 shorter events, 129.8 us)
Async XLA Ops:
  7.2 92.4 %all-gather.5.cloned.1.call-start = ((), (), s32[]{:S(2)}) async-start(), calls=%async_computation.6 | async-start | bytes 10485760 | tf_op jit(solution)/shard_map/all_gather | solution.py:159
  7.9 701.9 %all-gather.9.cloned.1.call-start = ((), (), s32[]{:S(2)}) async-start(), calls=%async_computation.8 | async-start | bytes 10485760 | tf_op jit(solution)/shard_map/all_gather | solution.py:175
  131.6 2.7 copy-start.3
  137.1 572.7 %all-gather.7.cloned.1.call-start = ((), (), s32[]{:S(2)}) async-start(), calls=%async_computation.7 | async-start | bytes 10485760 | tf_op jit(solution)/shard_map/all_gather | solution.py:174
  146.0 275.2 %all-to-all-start = ((bf16[3,4,256,1024]{3,2,0,1:T(8,128)(2,1)}), bf16[3,4,256,1024]{3,2,0,1:T(8,128)(2,1)}, u32[]{:S(2)}, u32[]{:S(2)}) async-start(bf16[3,4,256,1024]{3,2,0,1:T(8,128)(2,1)} %copy.98), calls=%async_computation | async-start | bytes 12582912 | tf_op jit(solution)/shard_map/all_to_all | solution.py:215
  478.6 42.4 %copy-start.1 = (f32[32,8,32,128]{3,2,1,0:T(8,128)S(1)}, f32[32,8,32,128]{3,2,1,0:T(8,128)}, u32[]{:S(2)}) copy-start(f32[32,8,32,128]{3,2,1,0:T(8,128)} %copy.140) | copy-start | bytes 12582916 | tf_op jit(solution)/shard_map/cond
  701.6 10.7 copy-start
  703.1 30.5 %all-to-all-start.1 = ((bf16[256,4,1024]{2,0,1:T(8,128)(2,1)}), bf16[256,4,1024]{2,0,1:T(8,128)(2,1)}, u32[]{:S(2)}, u32[]{:S(2)}) async-start(bf16[256,4,1024]{2,0,1:T(8,128)(2,1)} %bitcast.210), calls=%async_computation.1 | async-start | bytes 4194304 | tf_op jit(solution)/shard_map/all_to_all | solution.py:237
  707.5 248.7 %reduce-scatter.3.cloned.1.call-start = ((), (), s32[]{:S(2)}) async-start(), calls=%async_computation.9 | async-start | bytes 10485760 | tf_op jit(solution)/shard_map/reduce_scatter | solution.py:239
  750.2 303.5 %all-gather.11.cloned.1.call-start = ((), (), s32[]{:S(2)}) async-start(), calls=%async_computation.10 | async-start | bytes 10485760 | tf_op jit(solution)/shard_map/all_gather | solution.py:249
  956.3 6.3 collective-permute-start
  1067.4 1.3 copy-start.7
  1068.7 40.7 %all-to-all-start.2 = ((bf16[4,256,1024]{2,1,0:T(8,128)(2,1)}), bf16[4,256,1024]{2,1,0:T(8,128)(2,1)S(1)}, u32[]{:S(2)}, u32[]{:S(2)}) async-start(bf16[4,256,1024]{2,1,0:T(8,128)(2,1)} %bitcast.216), calls=%async_computation.3 | async-start | bytes 4194304 | tf_op jit(solution)/shard_map/all_to_all | solution.py:261
  1111.3 2.0 copy-start.2
  1135.7 3.0 copy-start.4
  1388.6 4.8 copy-start.6
  1409.8 99.1 %all-to-all-start.3 = ((bf16[3,256,4096]{1,0,2:T(4,128)(2,1)}), bf16[3,256,4096]{1,0,2:T(4,128)(2,1)}, u32[]{:S(2)}, u32[]{:S(2)}) async-start(bf16[3,256,4096]{1,0,2:T(4,128)(2,1)} %copy.113), calls=%async_computation.4 | async-start | bytes 16777216 | tf_op jit(solution)/shard_map/all_to_all | solution.py:281
  1415.5 236.9 %reduce-scatter.5.cloned.1.call-start = ((), (), s32[]{:S(2)}) async-start(), calls=%async_computation.11 | async-start | bytes 10485760 | tf_op jit(solution)/shard_map/reduce_scatter | solution.py:291
  1568.3 84.1 %copy-start.5 = (bf16[1024,1024]{0,1:T(8,128)(2,1)S(1)}, bf16[1024,1024]{0,1:T(8,128)(2,1)}, u32[]{:S(2)}) copy-start(bf16[1024,1024]{0,1:T(8,128)(2,1)} %reduce-scatter.3.cloned.1.call-done) | copy-start | bytes 6291460
  1570.2 3.6 collective-permute-start.1
Sparse Core Ops, SparseCore 0:
  9.8 89.6 all-gather.4
  137.2 284.1 all-gather.8
  422.9 170.0 all-gather.6
  750.3 205.9 reduce-scatter.2
  966.5 87.1 all-gather.10
  1568.4 83.9 reduce-scatter.4
where the time goes:
time: 1670 us; the launch traced here: 1660 us
  waiting for transfers between devices  880 us (53%)
  matrix products  436 us (26%)
  other arithmetic  188 us (11%)
  local copies, waits for them, and re-layouts  117 us (7%)
  starting transfers between devices  24.8 us (1%)
    all_to_all x1, waiting for transfers between devices, body(): lax.all_to_all(projected.reshape(3, seq_count, chan_count, row_count), 's...  264 us
    reduce_scatter x1, waiting for transfers between devices, body(): lax.psum_scatter(lax.dot_general(weights_out, mixed, (((0,), (0,)), ((),...  206 us
    dot_general x3, matrix products, forward_dft(): jnp.einsum('ckm,mj->ckj', jnp.concatenate([real_b, imag_b], axis=2), forw...  108 us
    dot_general x3, matrix products, inverse_dft(): jnp.einsum('ckm,mj->ckj', jnp.concatenate([real_x, imag_x], axis=2), inve...  101 us
    all_to_all x1, waiting for transfers between devices, body(): lax.all_to_all(d_fields, 'seq', split_axis=2, concat_axis=1, tiled=True)  93.4 us
    all_gather x1, waiting for transfers between devices, body(): lax.all_gather(seq_in, 'head', axis=1, tiled=True)  91.6 us
    all_gather x1, waiting for transfers between devices, body(): portion = lax.all_gather(diff, 'head', axis=0, tiled=True)  87.3 us
    reduce_scatter x1, waiting for transfers between devices, body(): lax.psum_scatter(lax.cond(teacher, skip_grad, make_grad, d_rows).astype(j...  75.3 us
  transfers between devices with their start and end apart: 12, of which 10 were waited for; matrix products, arithmetic and copies ran while one was open for 18% of the time, Pallas kernels for 0%

commit v1 on v0

v1 whole, which is shorter than its diff:
```python
import functools
import math

import jax
import jax.numpy as jnp
import numpy as np
from jax import lax
from jax.experimental import pallas as pl
from jax.experimental.pallas import tpu as pltpu
from jax.sharding import PartitionSpec as P

HD = 128
GROUP = 16
very_low = -1e30


def passed_along(value, axis, by):
    devices = lax.axis_size(axis)
    pairs = [(i, i + by) for i in range(devices) if 0 <= i + by < devices]
    return lax.ppermute(value, axis, pairs)


def dft_tables(length):
    total_len = 2 * length
    outer_len = total_len // 128
    half_len = outer_len // 2
    outer_idx = np.arange(outer_len)
    inner_idx = np.arange(128)
    outer = -2.0 * np.pi / outer_len * (outer_idx[:, None] * outer_idx[None, :] % outer_len)
    inner = -2.0 * np.pi / 128 * (inner_idx[:, None] * inner_idx[None, :] % 128)
    twist = -2.0 * np.pi / total_len * (outer_idx[:, None] * inner_idx[None, :] % total_len)
    cos_in, sin_in = np.cos(inner), np.sin(inner)
    first = np.concatenate([np.cos(outer)[:, :half_len], np.sin(outer)[:, :half_len]], axis=0)
    last = np.concatenate([np.cos(outer)[:half_len], np.sin(outer)[:half_len]], axis=1)
    first = np.kron(np.eye(max(1, 256 // half_len)), first)
    last = np.kron(np.eye(max(1, 256 // (2 * outer_len))), last)
    forward = np.block([[cos_in, sin_in], [-sin_in, cos_in]])
    inverse = np.block([[cos_in, -sin_in], [sin_in, cos_in]])
    narrow = [jnp.asarray(t, jnp.bfloat16) for t in (first, forward, inverse, last)]
    return (*narrow, jnp.asarray(np.cos(twist), jnp.float32), jnp.asarray(np.sin(twist), jnp.float32))


def product(a, b):
    return jnp.dot(a, b, preferred_element_type=jnp.float32)


def paired_rows(table, rows):
    depth = table.shape[1]
    out = []
    for at in range(0, rows.shape[0], 2 * depth):
        both = jnp.concatenate([rows[at : at + depth], rows[at + depth : at + 2 * depth]], axis=1)
        mixed = product(table, both)
        out += [mixed[:, :128], mixed[:, 128:]]
    return jnp.concatenate(out, axis=0)


def forward_dft(field, first, forward, cos_twist, sin_twist):
    channels, half_len, _ = field.shape
    outer_len = 2 * half_len
    rows = field.astype(jnp.bfloat16).reshape(channels * half_len, 128)
    mixed = paired_rows(first, rows).reshape(channels, 2 * outer_len, 128)
    real_a, imag_a = mixed[:, :outer_len], mixed[:, outer_len:]
    real_b = real_a * cos_twist - imag_a * sin_twist
    imag_b = real_a * sin_twist + imag_a * cos_twist
    both = jnp.concatenate([real_b, imag_b], axis=2).astype(jnp.bfloat16)
    spectrum = product(both.reshape(channels * outer_len, 256), forward)
    return spectrum[:, :128], spectrum[:, 128:]


def inverse_dft(real_x, imag_x, inverse, last, cos_twist, sin_twist):
    outer_len = cos_twist.shape[0]
    both = jnp.concatenate([real_x, imag_x], axis=1).astype(jnp.bfloat16)
    mixed = product(both, inverse)
    real_b = mixed[:, :128].reshape(-1, outer_len, 128)
    imag_b = mixed[:, 128:].reshape(-1, outer_len, 128)
    real_c = real_b * cos_twist + imag_b * sin_twist
    imag_c = imag_b * cos_twist - real_b * sin_twist
    rows = jnp.concatenate([real_c, imag_c], axis=1).astype(jnp.bfloat16)
    field = paired_rows(last, rows.reshape(-1, 128))
    return field.reshape(-1, outer_len // 2, 128)


def forward_kernel(
    scale, fields, filters, first, forward, inverse, last, cos_t, sin_t, gated, conv, spec_u, spec_h
):
    cos_twist, sin_twist = cos_t[...], sin_t[...]
    value_s = fields[0].astype(jnp.float32)
    gate_in = fields[1].astype(jnp.float32)
    gate_out = fields[2].astype(jnp.float32)
    real_u, imag_u = forward_dft(gate_in * value_s, first[...], forward[...], cos_twist, sin_twist)
    real_h, imag_h = forward_dft(filters[...], first[...], forward[...], cos_twist, sin_twist)
    spec_u[:, :128] = real_u.astype(spec_u.dtype)
    spec_u[:, 128:] = imag_u.astype(spec_u.dtype)
    spec_h[:, :128] = real_h.astype(spec_h.dtype)
    spec_h[:, 128:] = imag_h.astype(spec_h.dtype)
    out = scale * inverse_dft(
        real_u * real_h - imag_u * imag_h,
        real_u * imag_h + imag_u * real_h,
        inverse[...],
        last[...],
        cos_twist,
        sin_twist,
    )
    conv[...] = out
    gated[...] = (gate_out * out).astype(gated.dtype)


def backward_kernel(
    scale, fields, d_gated, conv, spec_u, spec_h, first, forward, inverse, last, cos_t, sin_t,
    d_fields, d_taps,
):
    cos_twist, sin_twist = cos_t[...], sin_t[...]
    grad = d_gated[...].astype(jnp.float32)
    d_fields[2] = (conv[...] * grad).astype(d_fields.dtype)
    d_conv = fields[2].astype(jnp.float32) * grad
    real_d, imag_d = forward_dft(d_conv, first[...], forward[...], cos_twist, sin_twist)

    def correlated(spec):
        real_s = spec[:, :128].astype(jnp.float32)
        imag_s = spec[:, 128:].astype(jnp.float32)
        return scale * inverse_dft(
            real_s * real_d + imag_s * imag_d,
            real_s * imag_d - imag_s * real_d,
            inverse[...],
            last[...],
            cos_twist,
            sin_twist,
        )

    d_carried = correlated(spec_h)
    d_fields[0] = (d_carried * fields[1].astype(jnp.float32)).astype(d_fields.dtype)
    d_fields[1] = (d_carried * fields[0].astype(jnp.float32)).astype(d_fields.dtype)
    d_taps[...] = correlated(spec_u)


def whole_spec(table):
    return pl.BlockSpec(table.shape, lambda i: (0, 0))


def student_specs(half_len):
    outer_len = 2 * half_len
    fields = pl.BlockSpec((3, GROUP, half_len, 128), lambda i: (0, i, 0, 0))
    single = pl.BlockSpec((GROUP, half_len, 128), lambda i: (i, 0, 0))
    spectrum = pl.BlockSpec((GROUP * outer_len, 256), lambda i: (i, 0))
    return fields, single, spectrum


def student_cost(channels, transforms):
    return pl.CostEstimate(
        flops=channels * transforms * 12_000_000,
        bytes_accessed=channels * transforms * 40_000,
        transcendentals=0,
    )


def student_forward(operands, tables, tap_scale):
    fields, filters = operands
    channels, length = filters.shape
    half_len = length // 128
    in_fields, single, spectrum = student_specs(half_len)
    scale = tap_scale / (2 * length)
    shape = (channels, half_len, 128)
    spec_shape = jax.ShapeDtypeStruct((channels * 2 * half_len, 256), jnp.bfloat16)
    gated, conv, spec_u, spec_h = pl.pallas_call(
        functools.partial(forward_kernel, scale),
        grid=(channels // GROUP,),
        in_specs=[in_fields, single, *map(whole_spec, tables)],
        out_specs=[single, single, spectrum, spectrum],
        out_shape=[
            jax.ShapeDtypeStruct(shape, jnp.bfloat16),
            jax.ShapeDtypeStruct(shape, jnp.float32),
            spec_shape,
            spec_shape,
        ],
        cost_estimate=student_cost(channels, 3),
        compiler_params=pltpu.CompilerParams(vmem_limit_bytes=48 * 2**20),
        name="student_forward",
    )(fields.reshape(3, *shape), filters.reshape(shape), *tables)
    return gated.reshape(channels, length), conv, spec_u, spec_h


def student_backward(operands, tables, tap_scale):
    fields, d_gated, conv, spec_u, spec_h = operands
    channels, length = d_gated.shape
    half_len = length // 128
    in_fields, single, spectrum = student_specs(half_len)
    scale = tap_scale / (2 * length)
    shape = (channels, half_len, 128)
    d_fields, d_taps = pl.pallas_call(
        functools.partial(backward_kernel, scale),
        grid=(channels // GROUP,),
        in_specs=[in_fields, single, single, spectrum, spectrum, *map(whole_spec, tables)],
        out_specs=[in_fields, single],
        out_shape=[
            jax.ShapeDtypeStruct((3, *shape), jnp.bfloat16),
            jax.ShapeDtypeStruct(shape, jnp.float32),
        ],
        cost_estimate=student_cost(channels, 3),
        compiler_params=pltpu.CompilerParams(vmem_limit_bytes=48 * 2**20),
        name="student_backward",
    )(fields.reshape(3, *shape), d_gated.reshape(shape), conv, spec_u, spec_h, *tables)
    return d_fields.reshape(3, channels, length), d_taps.reshape(channels, length)


def attend_kernel(block, factor, query, keys, values, out):
    at = pl.program_id(1)
    query_blk = query[0]

    def one_block(j, state, diagonal):
        highest, total, acc = state
        first = pl.multiple_of(j * block, block)
        scores = product(keys[0, pl.ds(first, block), :], query_blk)
        if diagonal:
            key_pos = lax.broadcasted_iota(jnp.int32, scores.shape, 0)
            query_pos = lax.broadcasted_iota(jnp.int32, scores.shape, 1)
            scores = jnp.where(key_pos <= query_pos, scores, -jnp.inf)
        new_max = jnp.maximum(highest, jnp.max(scores, axis=0, keepdims=True))
        expos = jnp.exp2((scores - new_max) * factor)
        fading = jnp.exp2((highest - new_max) * factor)
        total = total * fading + jnp.sum(expos, axis=0, keepdims=True)
        part = product(values[0, :, pl.ds(first, block)], expos.astype(jnp.bfloat16))
        return new_max, total, acc * fading + part

    state = (
        jnp.full((1, block), very_low, jnp.float32),
        jnp.zeros((1, block), jnp.float32),
        jnp.zeros((HD, block), jnp.float32),
    )
    state = lax.fori_loop(0, at, lambda j, inner: one_block(j, inner, False), state)
    _, total, acc = one_block(at, state, True)
    out[0] = (acc / total).astype(out.dtype)


def teacher_attend(fields):
    channels, length = fields.shape[1:]
    heads = channels // HD
    query, keys_t, values = fields.reshape(3, heads, HD, length)
    block = math.gcd(length, 512)
    pairs = heads * length * (length + block) // 2
    attended = pl.pallas_call(
        functools.partial(attend_kernel, block, HD ** (-0.5) * math.log2(math.e)),
        grid=(heads, length // block),
        in_specs=[
            pl.BlockSpec((1, HD, block), lambda h, i: (h, 0, i)),
            pl.BlockSpec((1, length, HD), lambda h, i: (h, 0, 0)),
            pl.BlockSpec((1, HD, length), lambda h, i: (h, 0, 0)),
        ],
        out_specs=pl.BlockSpec((1, HD, block), lambda h, i: (h, 0, i)),
        out_shape=jax.ShapeDtypeStruct((heads, HD, length), jnp.bfloat16),
        cost_estimate=pl.CostEstimate(
            flops=4 * HD * pairs, bytes_accessed=8 * channels * length, transcendentals=pairs
        ),
        compiler_params=pltpu.CompilerParams(vmem_limit_bytes=48 * 2**20),
        name="teacher_attend",
    )(query, keys_t.swapaxes(1, 2), values)
    return attended.reshape(channels, length)


def attend_gathered(projected, teacher):
    _, col_count, row_count = projected.shape
    head_count = col_count // HD
    parts = projected.reshape(3, head_count, HD, row_count)
    query = parts[0]
    first_row = lax.axis_index("seq") * row_count
    query_pos = first_row + jnp.arange(row_count, dtype=jnp.int32)
    factor = HD ** (-0.5)
    start_state = (
        jnp.full((head_count, row_count), very_low, jnp.float32),
        jnp.zeros((head_count, row_count), jnp.float32),
        jnp.zeros((head_count, HD, row_count), jnp.float32),
    )
    key_part = lax.all_gather(parts[1], "seq", axis=2, tiled=True)
    value_part = lax.all_gather(parts[2], "seq", axis=2, tiled=True)
    part_len = key_part.shape[2]
    step_len = math.gcd(part_len, 512)

    def one_block(block_no, status):
        offset = block_no * step_len
        key_blk = lax.dynamic_slice_in_dim(key_part, offset, step_len, 2)
        value_blk = lax.dynamic_slice_in_dim(value_part, offset, step_len, 2)
        key_pos = offset + jnp.arange(step_len, dtype=jnp.int32)

        def attend(inner):
            running_max, running_sum, running_acc = inner
            scores = (
                jnp.einsum("hdi,hdj->hij", query, key_blk, preferred_element_type=jnp.float32)
                * factor
            )
            scores = jnp.where(key_pos[None, None, :] <= query_pos[None, :, None], scores, -jnp.inf)
            new_max = jnp.maximum(running_max, jnp.max(scores, axis=2))
            expos = jnp.exp(scores - new_max[:, :, None])
            fading = jnp.exp(running_max - new_max)
            new_sum = running_sum * fading + jnp.sum(expos, axis=2)
            product = jnp.einsum(
                "hij,hdj->hdi",
                expos.astype(jnp.bfloat16),
                value_blk,
                preferred_element_type=jnp.float32,
            )
            return (new_max, new_sum, running_acc * fading[:, None, :] + product)

        def keep(inner):
            return inner

        return lax.cond(teacher, attend, keep, status)

    final_max, final_sum, final_acc = lax.fori_loop(0, part_len // step_len, one_block, start_state)
    attended = (
        (final_acc / jnp.where(teacher, final_sum, 1.0)[:, None, :])
        .reshape(col_count, row_count)
        .astype(jnp.bfloat16)
    )
    return attended


def body(seq_in, w_proj, w_out, filters):
    teacher = lax.axis_index("grp") == 0
    row_count = seq_in.shape[0]
    weights_in = w_proj[0]
    weights_out = w_out[0]
    col_count = weights_in.shape[2]
    seq_count = lax.axis_size("seq")
    chan_count = col_count // seq_count
    length = row_count * seq_count
    outer_len = 2 * length // 128
    tap_scale = length ** (-0.5)
    block = weights_in
    projected = lax.dot_general(
        block,
        lax.all_gather(seq_in, "head", axis=1, tiled=True),
        (((1,), (1,)), ((), ())),
        preferred_element_type=jnp.float32,
    ).astype(jnp.bfloat16)
    projected = projected.reshape(3, col_count, row_count)
    by_heads = chan_count % HD == 0
    spread = lax.all_to_all(
        projected.reshape(3, seq_count, chan_count, row_count),
        "seq",
        split_axis=1,
        concat_axis=3,
        tiled=True,
    )
    fields_c = spread.reshape(3, chan_count, length)
    tables = dft_tables(length)

    def run_student(operands):
        return student_forward(operands, tables, tap_scale)

    def run_teacher(operands):
        spec = jnp.zeros((chan_count * outer_len, 256), jnp.bfloat16)
        if by_heads:
            attended = teacher_attend(operands[0])
        else:
            attended = jnp.zeros((chan_count, length), jnp.bfloat16)
        conv = jnp.zeros((chan_count, length // 128, 128), jnp.float32)
        return attended, conv, spec, spec

    mixed, conv, spec_u, spec_h = lax.cond(teacher, run_teacher, run_student, (fields_c, filters))
    mixed = lax.all_to_all(mixed, "seq", split_axis=1, concat_axis=0, tiled=True)
    if not by_heads:
        mixed = jnp.where(teacher, attend_gathered(projected, teacher), mixed)
    y_own = lax.psum_scatter(
        lax.dot_general(
            weights_out, mixed, (((0,), (0,)), ((), ())), preferred_element_type=jnp.float32
        ).astype(jnp.bfloat16),
        "head",
        scatter_dimension=0,
        tiled=True,
    )
    target = passed_along(y_own, "grp", 1)
    diff = (y_own.astype(jnp.float32) - target.astype(jnp.float32)).astype(jnp.bfloat16)
    portion = lax.all_gather(diff, "head", axis=0, tiled=True)
    block = weights_out

    def keep_sum(current):
        return current

    def grow_sum(current):
        return jnp.dot(block, portion, preferred_element_type=jnp.float32)

    d_gated = lax.cond(
        teacher, keep_sum, grow_sum, jnp.zeros((col_count, row_count), jnp.float32)
    ).astype(jnp.bfloat16)
    d_spread = lax.all_to_all(
        d_gated.reshape(seq_count, chan_count, row_count),
        "seq",
        split_axis=0,
        concat_axis=2,
        tiled=True,
    ).reshape(chan_count, length)

    def run_backward(operands):
        return student_backward(operands, tables, tap_scale)

    def spare_backward(operands):
        return (
            jnp.zeros((3, chan_count, length), jnp.bfloat16),
            jnp.zeros((chan_count, length), jnp.float32),
        )

    d_fields, d_taps = lax.cond(
        teacher, spare_backward, run_backward, (fields_c, d_spread, conv, spec_u, spec_h)
    )
    d_rows = lax.all_to_all(d_fields, "seq", split_axis=2, concat_axis=1, tiled=True)

    def skip_grad(operand):
        return jnp.zeros((lax.axis_size("head") * col_count, row_count), jnp.float32)

    def make_grad(operand):
        return lax.dot_general(
            weights_in, operand, (((0, 2), (0, 1)), ((), ())), preferred_element_type=jnp.float32
        )

    d_input = lax.psum_scatter(
        lax.cond(teacher, skip_grad, make_grad, d_rows).astype(jnp.bfloat16),
        "head",
        scatter_dimension=0,
        tiled=True,
    )
    paired = jnp.where(teacher, y_own.T, d_input.T)[None]
    half_len = length // 2
    lower_taps = passed_along(d_taps[:, :half_len].astype(jnp.bfloat16), "grp", -1).astype(
        jnp.float32
    )
    grad_filters = jnp.where(teacher, lower_taps, d_taps[:, half_len:])
    return (paired, grad_filters)


def solution(mesh):
    return jax.shard_map(
        body,
        mesh=mesh,
        in_specs=(
            P("seq", "head"),
            P("grp", None, None, "head"),
            P("grp", "head", None),
            P(("head", "seq"), None),
        ),
        out_specs=(P("grp", "seq", "head"), P(("head", "seq"), "grp")),
        check_vma=False,
    )
```

time: 1670 us -> 1020 us (0.61)
  matrix products: 436 us -> 93 us
  waiting for transfers between devices: 880 us -> 681 us
  other arithmetic: 188 us -> 10.3 us
  Pallas kernels: 0 us -> 49.6 us
  blocking collectives: 0 us -> 29.2 us
    dot_general x15 -> x0, matrix products: 343 us -> none  [the longest x3 108 us: forward_dft(): jnp.einsum('ckm,mj->ckj', jnp.concatenate([real_b, imag_b], axis=2), forw...]
    all_to_all x1, waiting for transfers between devices: 264 us -> 138 us  [body(): lax.all_to_all(projected.reshape(3, seq_count, chan_count, row_count), 's...]
    reduce_scatter x1, waiting for transfers between devices: 206 us -> 122 us  [body(): lax.psum_scatter(lax.dot_general(weights_out, mixed, (((0,), (0,)), ((),...]
    add x4 -> x0, other arithmetic: 73.9 us -> none  [the longest x1 29.3 us: student_backward(): real_u * real_d + imag_u * imag_d]
    pallas_call x0 -> x2, Pallas kernels: none -> 49.6 us  [the longest x1 27.4 us: student_backward(): pl.pallas_call(functools.partial(backward_kernel, scale), grid=(channels...]
    concatenate x8 -> x0, other arithmetic: 42.5 us -> none  [the longest x3 29.2 us: forward_dft(): jnp.concatenate([real_b, imag_b], axis=2)]
    all_to_all x1, waiting for transfers between devices: 93.4 us -> 123 us  [body(): lax.all_to_all(d_fields, 'seq', split_axis=2, concat_axis=1, tiled=True)]
    all_to_all x0 -> x1, blocking collectives: none -> 29.2 us  [body(): lax.all_to_all(mixed, 'seq', split_axis=1, concat_axis=0, tiled=True)]
  transfers between devices with their start and end apart: 12 -> 9, of which waited for: 10 -> 9; matrix products, arithmetic and copies ran while one was open for 18% -> 1% of each run, Pallas kernels for 0% -> 0%
where the time goes in v1:
time: 1020 us; the launch traced here: 1010 us
  waiting for transfers between devices  681 us (67%)
  local copies, waits for them, and re-layouts  116 us (11%)
  matrix products  93 us (9%)
  Pallas kernels  49.6 us (5%)
  blocking collectives  29.2 us (3%)
  starting transfers between devices  18 us (2%)
  between operations  14.4 us (1%)
  other arithmetic  10.3 us (1%)
    all_to_all x1, waiting for transfers between devices, body(): lax.all_to_all(projected.reshape(3, seq_count, chan_count, row_count), 's...  138 us
    all_to_all x1, waiting for transfers between devices, body(): lax.all_to_all(d_fields, 'seq', split_axis=2, concat_axis=1, tiled=True)  123 us
    reduce_scatter x1, waiting for transfers between devices, body(): lax.psum_scatter(lax.dot_general(weights_out, mixed, (((0,), (0,)), ((),...  122 us
    all_gather x1, waiting for transfers between devices, body(): lax.all_gather(seq_in, 'head', axis=1, tiled=True)  91.7 us
    all_gather x1, waiting for transfers between devices, body(): portion = lax.all_gather(diff, 'head', axis=0, tiled=True)  87.2 us
    reduce_scatter x1, waiting for transfers between devices, body(): lax.psum_scatter(lax.cond(teacher, skip_grad, make_grad, d_rows).astype(j...  75.3 us
    all_to_all x1, waiting for transfers between devices, body(): lax.all_to_all(d_gated.reshape(seq_count, chan_count, row_count), 'seq',...  36.4 us
    dot_general x1, matrix products, make_grad(): lax.dot_general(weights_in, operand, (((0, 2), (0, 1)), ((), ())), prefer...  32.6 us
  transfers between devices with their start and end apart: 9, of which 9 were waited for; matrix products, arithmetic and copies ran while one was open for 1% of the time, Pallas kernels for 0%

profile of v1, /device:TPU:1, one launch (start us, length us, event | category | flops | bytes accessed | tf_op | source)
XLA Modules:
  0.0 1012.4 jit_solution(1627177064724702287)
XLA Ops:
  7.9 91.7 %all-gather.3.cloned.1.call-done = bf16[1024,4096]{1,0:T(8,128)(2,1)} async-done(((bf16[1024,1024]{1,0:T(8,128)(2,1)}), bf16[1024,4096]{1,0:T(8,128)(2,1)}) %all-gather.3.cloned.1.call-update) | async-done | bytes 8388624 | tf_op jit(solution)/shard_map/all_gather | solution.py:330
  99.6 32.1 %fusion.2 = bf16[3,1024,1024]{2,1,0:T(8,128)(2,1)S(1)} fusion(bf16[1024,4096]{1,0:T(8,128)(2,1)} %all-gather.3.cloned.1.call-done, bf16[1,3,4096,1024]{3,2,1,0:T(8,128)(2,1)} %param.19), kind=kOutput, calls=%fused_computation.7 | convolution fusion | flops 25772949504 | bytes 39845888 | tf_op jit(solution)/shard_map/dot_general | solution.py:328
  131.6 3.3 copy.52
  135.0 5.3 all-to-all-start
  140.4 137.5 %all-to-all-done = bf16[3,4,256,1024]{3,2,0,1:T(8,128)(2,1)} async-done(((bf16[3,4,256,1024]{3,2,0,1:T(8,128)(2,1)}), bf16[3,4,256,1024]{3,2,0,1:T(8,128)(2,1)}, u32[]{:S(2)}, u32[]{:S(2)}) %all-to-all-start) | async-done | bytes 6291488 | tf_op jit(solution)/shard_map/all_to_all | solution.py:336
  277.9 8.6 copy.53
  286.6 38.7 %conditional.4 = (bf16[256,4096]{1,0:T(8,128)(2,1)}, f32[256,32,128]{2,1,0:T(8,128)S(1)}, bf16[16384,256]{1,0:T(8,128)(2,1)S(1)}, bf16[16384,256]{1,0:T(8,128)(2,1)}) conditional(s32[]{:T(128)} %convert_element_type.34, (bf16[3,1,256,4096]{2,3,0,1:T(8,128)(2,1)}, f32[256,4096]{1,0:T(8,128)}, bf16[1024,256]{1,0:T(8,128)(2,1)S(1)}, ...), branch_computations={%region_0.0_spmd, %region_1.0_spmd} | conditional | flops 9663676416 | bytes 67108928 | solution.py:358
  286.6 5.0 copy.70
  291.6 9.1 copy.67.fields
  300.7 22.2 %student_forward.1 = (bf16[256,32,128]{2,1,0:T(8,128)(2,1)S(1)}, f32[256,32,128]{2,1,0:T(8,128)S(1)}, bf16[16384,256]{1,0:T(8,128)(2,1)S(1)}, bf16[16384,256]{1,0:T(8,128)(2,1)}) custom-call(bf16[3,256,32,128]{3,2,1,0:T(8,128)(2,1)} %copy.67.fields, f32[256,32,128]{2,1,0:T(8,128)} %bitcast.76, bf16[1024,256]{1,0:T(8,128)(2,1)S(1)} %get-tuple-element.57.first, ...), custom_call_target="tpu_custom_call" | custom-call | flops 9216000000 | bytes 30720000 | tf_op jit(solution)/shard_map/cond/branch_0_fun/student_forward/pallas_call | solution.py:164
  322.9 2.3 copy.75
  325.4 3.2 copy-done.3
  328.6 2.0 copy-done.4
  330.6 3.3 copy.56
  333.8 29.2 %all_to_all.74 = bf16[256,4,1024]{0,2,1:T(8,128)(2,1)} all-to-all(bf16[256,4,1024]{0,2,1:T(8,128)(2,1)S(1)} %bitcast.70), channel_id=1, replica_groups=mesh['grp'=2,'head'=4,'seq'=4] {'seq'}, dimensions={1} | all-to-all | bytes 4194304 | tf_op jit(solution)/shard_map/all_to_all | solution.py:359
  363.1 3.0 copy.57
  366.1 14.6 %convert_bitcast_fusion = bf16[4096,1024]{0,1:T(8,128)(2,1)} fusion(bf16[1024,1024]{1,0:T(8,128)(2,1)S(1)} %bitcast.78, bf16[1,1024,4096]{2,1,0:T(8,128)(2,1)} %param.20), kind=kOutput, calls=%fused_computation.5 | convolution fusion | flops 8594128896 | bytes 18874368 | tf_op jit(solution)/shard_map/dot_general | solution.py:363
  380.7 121.8 %reduce-scatter.3.cloned.1.call-done = bf16[1024,1024]{0,1:T(8,128)(2,1)} async-done(((bf16[4096,1024]{0,1:T(8,128)(2,1)}), bf16[1024,1024]{0,1:T(8,128)(2,1)}) %reduce-scatter.3.cloned.1.call-update) | async-done | bytes 2097168 | tf_op jit(solution)/shard_map/reduce_scatter | solution.py:362
  502.5 1.3 collective-permute-start
  503.8 5.0 collective-permute-done
  508.8 3.9 subtract_convert_fusion
  512.7 87.2 %all-gather.5.cloned.1.call-done = bf16[4096,1024]{0,1:T(8,128)(2,1)} async-done(((bf16[1024,1024]{0,1:T(8,128)(2,1)}), bf16[4096,1024]{0,1:T(8,128)(2,1)}) %all-gather.5.cloned.1.call-update) | async-done | bytes 8388624 | tf_op jit(solution)/shard_map/all_gather | solution.py:372
  599.9 13.7 %conditional.5 = (bf16[1024,1024]{1,0:T(8,128)(2,1)S(1)}) conditional(s32[]{:T(128)} %convert_element_type.34, (bf16[1024,4096]{1,0:T(8,128)(2,1)}, bf16[4096,1024]{0,1:T(8,128)(2,1)}) %tuple.83, () %tuple.38), branch_computations={%region_3.0_spmd, %region_4.0_spmd} | conditional | flops 8589934592 | bytes 18874376 | solution.py:381
  599.9 13.7 %fusion.8 = bf16[1024,1024]{1,0:T(8,128)(2,1)S(1)} fusion(bf16[1024,4096]{1,0:T(8,128)(2,1)} %get-tuple-element.67, bf16[4096,1024]{0,1:T(8,128)(2,1)} %get-tuple-element.156), kind=kOutput, calls=%fused_computation.14 | convolution fusion | flops 8589934592 | bytes 18874368 | tf_op jit(solution)/shard_map/cond/branch_0_fun/dot_general | solution.py:379
  613.7 1.3 copy-done.2
  615.0 4.3 all-to-all-start.2
  619.3 36.4 %all-to-all-done.2 = bf16[4,256,1024]{2,1,0:T(8,128)(2,1)S(1)} async-done(((bf16[4,256,1024]{2,1,0:T(8,128)(2,1)}), bf16[4,256,1024]{2,1,0:T(8,128)(2,1)S(1)}, u32[]{:S(2)}, u32[]{:S(2)}) %all-to-all-start.2) | async-done | bytes 2097184 | tf_op jit(solution)/shard_map/all_to_all | solution.py:384
  655.7 60.6 %conditional.6 = (bf16[3,256,4096]{2,1,0:T(8,128)(2,1)}, f32[256,4096]{1,0:T(8,128)}) conditional(s32[]{:T(128)} %convert_element_type.34, (bf16[3,1,256,4096]{2,3,0,1:T(8,128)(2,1)}, bf16[1,256,4,1024]{3,1,2,0:T(8,128)(2,1)S(1)}, f32[256,32,128]{2,1,0:T(8,128)}, bf16[16384,256]{1,0:T(8,128)(2,1)}, bf16[16384,256]{1,0:T(8,128)(2,1)}, ...), branch_computations={%region_5.0_spmd, %region_6.0_spmd} | conditional | flops 9216000000 | bytes 72663056 | solution.py:401
  655.9 2.9 copy.60
  658.9 2.7 reshape_reshape.9.d_gated
  661.6 9.0 copy.68.fields
  670.6 27.4 %student_backward.1 = (bf16[3,256,32,128]{3,2,1,0:T(8,128)(2,1)}, f32[256,32,128]{2,1,0:T(8,128)}) custom-call(bf16[3,256,32,128]{3,2,1,0:T(8,128)(2,1)} %copy.68.fields, bf16[256,32,128]{2,1,0:T(8,128)(2,1)S(1)} %reshape_reshape.9.d_gated, f32[256,32,128]{2,1,0:T(8,128)} %get-tuple-element.71.conv, bf16[16384,256]{1,0:T(8,128)(2,1)} %get-tuple-element.72.spec_u, ...), custom_call_target="tpu_custom_call" | custom-call | flops 9216000000 | bytes 30720000 | tf_op jit(solution)/shard_map/cond/branch_0_fun/student_backward/pallas_call | solution.py:189
  698.0 10.3 %reshape.31 = bf16[3,256,4096]{2,1,0:T(8,128)(2,1)} reshape(bf16[3,256,32,128]{3,2,1,0:T(8,128)(2,1)} %get-tuple-element.80) | data formatting | bytes 12582912 | tf_op jit(solution)/shard_map/cond/branch_0_fun/reshape | solution.py:202
  708.3 7.9 copy.76
  716.3 13.1 %copy.61 = bf16[3,256,4096]{1,0,2:T(4,128)(2,1)} copy(bf16[3,256,4096]{2,1,0:T(8,128)(2,1)} %get-tuple-element.96) | data formatting | bytes 12582912 | tf_op jit(solution)/shard_map/cond | solution.py:401
  729.4 5.6 all-to-all-start.3
  735.1 123.5 %all-to-all-done.3 = bf16[3,256,4096]{1,0,2:T(4,128)(2,1)} async-done(((bf16[3,256,4096]{1,0,2:T(4,128)(2,1)}), bf16[3,256,4096]{1,0,2:T(4,128)(2,1)}, u32[]{:S(2)}, u32[]{:S(2)}) %all-to-all-start.3) | async-done | bytes 6291488 | tf_op jit(solution)/shard_map/all_to_all | solution.py:404
  858.5 6.9 copy.62
  865.4 41.5 %conditional.7 = (bf16[4096,1024]{1,0:T(8,128)(2,1)}) conditional(s32[]{:T(128)} %convert_element_type.34, (bf16[3,4,256,1024]{2,3,1,0:T(8,128)(2,1)}, bf16[3,4096,1024]{2,1,0:T(8,128)(2,1)}) %tuple.82, () %tuple.42), branch_computations={%region_7.0_spmd, %region_8.0_spmd} | conditional | flops 25769803776 | bytes 52428808 | solution.py:415
  865.7 8.6 copy.63
  874.3 32.6 %convolution_bitcast_fusion = bf16[4096,1024]{1,0:T(8,128)(2,1)} fusion(bf16[3,4096,1024]{2,1,0:T(8,128)(2,1)} %get-tuple-element.82, bf16[3,1024,1024]{2,1,0:T(8,128)(2,1)} %bitcast.74), kind=kOutput, calls=%fused_computation.2 | convolution fusion | flops 25769803776 | bytes 39845888 | tf_op jit(solution)/shard_map/cond/branch_0_fun/dot_general | solution.py:410
  906.9 11.3 %copy.64 = bf16[4096,1024]{0,1:T(8,128)(2,1)} copy(bf16[4096,1024]{1,0:T(8,128)(2,1)} %get-tuple-element.187) | data formatting | bytes 16777216 | tf_op jit(solution)/shard_map/cond | solution.py:415
  918.2 1.9 slice.15
  920.1 1.4 collective-permute-start.1
  921.5 2.2 collective-permute-done.1
  923.7 3.3 slice_select_fusion
  927.0 75.3 %reduce-scatter.5.cloned.1.call-done = bf16[1024,1024]{0,1:T(8,128)(2,1)} async-done(((bf16[4096,1024]{0,1:T(8,128)(2,1)}), bf16[1024,1024]{0,1:T(8,128)(2,1)}) %reduce-scatter.5.cloned.1.call-update) | async-done | bytes 2097168 | tf_op jit(solution)/shard_map/reduce_scatter | solution.py:414
  1002.3 3.1 select_bitcast_fusion
  (25 shorter events, 0.9 us)
Async XLA Ops:
  7.2 92.4 %all-gather.3.cloned.1.call-start = ((), (), s32[]{:S(2)}) async-start(), calls=%async_computation.6 | async-start | bytes 10485760 | tf_op jit(solution)/shard_map/all_gather | solution.py:330
  135.0 142.9 %all-to-all-start = ((bf16[3,4,256,1024]{3,2,0,1:T(8,128)(2,1)}), bf16[3,4,256,1024]{3,2,0,1:T(8,128)(2,1)}, u32[]{:S(2)}, u32[]{:S(2)}) async-start(bf16[3,4,256,1024]{3,2,0,1:T(8,128)(2,1)} %copy.52), calls=%async_computation | async-start | bytes 12582912 | tf_op jit(solution)/shard_map/all_to_all | solution.py:336
  140.2 362.3 %reduce-scatter.3.cloned.1.call-start = ((), (), s32[]{:S(2)}) async-start(), calls=%async_computation.7 | async-start | bytes 10485760 | tf_op jit(solution)/shard_map/reduce_scatter | solution.py:362
  140.3 146.3 %copy-start.5 = (bf16[1024,256]{1,0:T(8,128)(2,1)S(1)}, bf16[1024,256]{1,0:T(8,128)(2,1)}, u32[]{:S(2)}) copy-start(bf16[1024,256]{1,0:T(8,128)(2,1)} %constant.32.clone) | copy-start | bytes 1572868
  140.3 146.3 %copy-start.6 = (bf16[256,256]{1,0:T(8,128)(2,1)S(1)}, bf16[256,256]{1,0:T(8,128)(2,1)}, u32[]{:S(2)}) copy-start(bf16[256,256]{1,0:T(8,128)(2,1)} %constant.34.clone) | copy-start | bytes 393220
  140.3 146.2 %copy-start.7 = (bf16[256,256]{1,0:T(8,128)(2,1)S(1)}, bf16[256,256]{1,0:T(8,128)(2,1)}, u32[]{:S(2)}) copy-start(bf16[256,256]{1,0:T(8,128)(2,1)} %constant.33.clone) | copy-start | bytes 393220
  140.3 146.2 %copy-start.8 = (f32[64,128]{1,0:T(8,128)S(1)}, f32[64,128]{1,0:T(8,128)}, u32[]{:S(2)}) copy-start(f32[64,128]{1,0:T(8,128)} %constant.37.clone) | copy-start | bytes 98308
  140.3 146.2 %copy-start.9 = (f32[64,128]{1,0:T(8,128)S(1)}, f32[64,128]{1,0:T(8,128)}, u32[]{:S(2)}) copy-start(f32[64,128]{1,0:T(8,128)} %constant.36.clone) | copy-start | bytes 98308
  140.4 146.2 %copy-start.10 = (bf16[64,256]{1,0:T(8,128)(2,1)S(1)}, bf16[64,256]{1,0:T(8,128)(2,1)}, u32[]{:S(2)}) copy-start(bf16[64,256]{1,0:T(8,128)(2,1)} %constant.35.clone) | copy-start | bytes 98308
  325.3 3.3 copy-start.3
  328.6 2.0 copy-start.4
  380.7 219.3 %all-gather.5.cloned.1.call-start = ((), (), s32[]{:S(2)}) async-start(), calls=%async_computation.8 | async-start | bytes 10485760 | tf_op jit(solution)/shard_map/all_gather | solution.py:372
  502.5 6.3 collective-permute-start
  613.7 1.3 copy-start.2
  615.0 40.7 %all-to-all-start.2 = ((bf16[4,256,1024]{2,1,0:T(8,128)(2,1)}), bf16[4,256,1024]{2,1,0:T(8,128)(2,1)S(1)}, u32[]{:S(2)}, u32[]{:S(2)}) async-start(bf16[4,256,1024]{2,1,0:T(8,128)(2,1)} %bitcast.79), calls=%async_computation.3 | async-start | bytes 4194304 | tf_op jit(solution)/shard_map/all_to_all | solution.py:384
  729.4 129.1 %all-to-all-start.3 = ((bf16[3,256,4096]{1,0,2:T(4,128)(2,1)}), bf16[3,256,4096]{1,0,2:T(4,128)(2,1)}, u32[]{:S(2)}, u32[]{:S(2)}) async-start(bf16[3,256,4096]{1,0,2:T(4,128)(2,1)} %copy.61), calls=%async_computation.4 | async-start | bytes 16777216 | tf_op jit(solution)/shard_map/all_to_all | solution.py:404
  735.0 267.3 %reduce-scatter.5.cloned.1.call-start = ((), (), s32[]{:S(2)}) async-start(), calls=%async_computation.9 | async-start | bytes 10485760 | tf_op jit(solution)/shard_map/reduce_scatter | solution.py:414
  918.2 84.1 %copy-start.1 = (bf16[1024,1024]{0,1:T(8,128)(2,1)S(1)}, bf16[1024,1024]{0,1:T(8,128)(2,1)}, u32[]{:S(2)}) copy-start(bf16[1024,1024]{0,1:T(8,128)(2,1)} %reduce-scatter.3.cloned.1.call-done) | copy-start | bytes 6291460
  920.1 3.6 collective-permute-start.1
Sparse Core Ops, SparseCore 0:
  9.8 89.6 all-gather.2
  380.8 121.7 reduce-scatter.2
  512.8 87.0 all-gather.4
  918.4 83.8 reduce-scatter.4

commit v2 on v1

--- a/solution.py
+++ b/solution.py
@@ -80,13 +80,23 @@
     return field.reshape(-1, outer_len // 2, 128)
 
 
+def joined(ref, *at):
+    blocks = ref.shape[len(at)]
+    parts = [ref[(*at, b)].astype(jnp.float32) for b in range(blocks)]
+    return jnp.concatenate(parts, axis=1)
+
+
+def scatter_to(ref, value, *at):
+    share = ref.shape[-2]
+    for b in range(ref.shape[0]):
+        ref[(b, *at)] = value[:, b * share : (b + 1) * share].astype(ref.dtype)
+
+
 def forward_kernel(
     scale, fields, filters, first, forward, inverse, last, cos_t, sin_t, gated, conv, spec_u, spec_h
 ):
     cos_twist, sin_twist = cos_t[...], sin_t[...]
-    value_s = fields[0].astype(jnp.float32)
-    gate_in = fields[1].astype(jnp.float32)
-    gate_out = fields[2].astype(jnp.float32)
+    value_s, gate_in, gate_out = joined(fields, 0), joined(fields, 1), joined(fields, 2)
     real_u, imag_u = forward_dft(gate_in * value_s, first[...], forward[...], cos_twist, sin_twist)
     real_h, imag_h = forward_dft(filters[...], first[...], forward[...], cos_twist, sin_twist)
     spec_u[:, :128] = real_u.astype(spec_u.dtype)
@@ -102,7 +112,7 @@
         sin_twist,
     )
     conv[...] = out
-    gated[...] = (gate_out * out).astype(gated.dtype)
+    scatter_to(gated, gate_out * out)
 
 
 def backward_kernel(
@@ -110,9 +120,9 @@
     d_fields, d_taps,
 ):
     cos_twist, sin_twist = cos_t[...], sin_t[...]
-    grad = d_gated[...].astype(jnp.float32)
-    d_fields[2] = (conv[...] * grad).astype(d_fields.dtype)
-    d_conv = fields[2].astype(jnp.float32) * grad
+    grad = joined(d_gated)
+    scatter_to(d_fields, conv[...] * grad, 2)
+    d_conv = joined(fields, 2) * grad
     real_d, imag_d = forward_dft(d_conv, first[...], forward[...], cos_twist, sin_twist)
 
     def correlated(spec):
@@ -128,8 +138,8 @@
         )
 
     d_carried = correlated(spec_h)
-    d_fields[0] = (d_carried * fields[1].astype(jnp.float32)).astype(d_fields.dtype)
-    d_fields[1] = (d_carried * fields[0].astype(jnp.float32)).astype(d_fields.dtype)
+    scatter_to(d_fields, d_carried * joined(fields, 1), 0)
+    scatter_to(d_fields, d_carried * joined(fields, 0), 1)
     d_taps[...] = correlated(spec_u)
 
 
@@ -137,12 +147,15 @@
     return pl.BlockSpec(table.shape, lambda i: (0, 0))
 
 
-def student_specs(half_len):
+def student_specs(half_len, blocks):
     outer_len = 2 * half_len
-    fields = pl.BlockSpec((3, GROUP, half_len, 128), lambda i: (0, i, 0, 0))
+    share = half_len // blocks
+    fields = pl.BlockSpec((3, blocks, GROUP, share, 128), lambda i: (0, 0, i, 0, 0))
+    d_fields = pl.BlockSpec((blocks, 3, GROUP, share, 128), lambda i: (0, 0, i, 0, 0))
+    spread = pl.BlockSpec((blocks, GROUP, share, 128), lambda i: (0, i, 0, 0))
     single = pl.BlockSpec((GROUP, half_len, 128), lambda i: (i, 0, 0))
     spectrum = pl.BlockSpec((GROUP * outer_len, 256), lambda i: (i, 0))
-    return fields, single, spectrum
+    return fields, d_fields, spread, single, spectrum
 
 
 def student_cost(channels, transforms):
@@ -157,17 +170,19 @@
     fields, filters = operands
     channels, length = filters.shape
     half_len = length // 128
-    in_fields, single, spectrum = student_specs(half_len)
+    blocks = fields.shape[1]
+    in_fields, _, spread, single, spectrum = student_specs(half_len, blocks)
     scale = tap_scale / (2 * length)
     shape = (channels, half_len, 128)
+    split = (blocks, channels, half_len // blocks, 128)
     spec_shape = jax.ShapeDtypeStruct((channels * 2 * half_len, 256), jnp.bfloat16)
     gated, conv, spec_u, spec_h = pl.pallas_call(
         functools.partial(forward_kernel, scale),
         grid=(channels // GROUP,),
         in_specs=[in_fields, single, *map(whole_spec, tables)],
-        out_specs=[single, single, spectrum, spectrum],
+        out_specs=[spread, single, spectrum, spectrum],
         out_shape=[
-            jax.ShapeDtypeStruct(shape, jnp.bfloat16),
+            jax.ShapeDtypeStruct(split, jnp.bfloat16),
             jax.ShapeDtypeStruct(shape, jnp.float32),
             spec_shape,
             spec_shape,
@@ -175,34 +190,36 @@
         cost_estimate=student_cost(channels, 3),
         compiler_params=pltpu.CompilerParams(vmem_limit_bytes=48 * 2**20),
         name="student_forward",
-    )(fields.reshape(3, *shape), filters.reshape(shape), *tables)
-    return gated.reshape(channels, length), conv, spec_u, spec_h
+    )(fields.reshape(3, *split), filters.reshape(shape), *tables)
+    return gated.reshape(blocks, channels, -1), conv, spec_u, spec_h
 
 
 def student_backward(operands, tables, tap_scale):
     fields, d_gated, conv, spec_u, spec_h = operands
-    channels, length = d_gated.shape
+    blocks, channels, rows = d_gated.shape
+    length = blocks * rows
     half_len = length // 128
-    in_fields, single, spectrum = student_specs(half_len)
+    in_fields, out_fields, spread, single, spectrum = student_specs(half_len, blocks)
     scale = tap_scale / (2 * length)
     shape = (channels, half_len, 128)
+    split = (blocks, channels, half_len // blocks, 128)
     d_fields, d_taps = pl.pallas_call(
         functools.partial(backward_kernel, scale),
         grid=(channels // GROUP,),
-        in_specs=[in_fields, single, single, spectrum, spectrum, *map(whole_spec, tables)],
-        out_specs=[in_fields, single],
+        in_specs=[in_fields, spread, single, spectrum, spectrum, *map(whole_spec, tables)],
+        out_specs=[out_fields, single],
         out_shape=[
-            jax.ShapeDtypeStruct((3, *shape), jnp.bfloat16),
+            jax.ShapeDtypeStruct((blocks, 3, *split[1:]), jnp.bfloat16),
             jax.ShapeDtypeStruct(shape, jnp.float32),
         ],
         cost_estimate=student_cost(channels, 3),
         compiler_params=pltpu.CompilerParams(vmem_limit_bytes=48 * 2**20),
         name="student_backward",
-    )(fields.reshape(3, *shape), d_gated.reshape(shape), conv, spec_u, spec_h, *tables)
-    return d_fields.reshape(3, channels, length), d_taps.reshape(channels, length)
-
-
-def attend_kernel(block, factor, query, keys, values, out):
+    )(fields.reshape(3, *split), d_gated.reshape(split), conv, spec_u, spec_h, *tables)
+    return d_fields, d_taps.reshape(channels, length)
+
+
+def attend_kernel(block, per, factor, query, keys, values, out):
     at = pl.program_id(1)
     query_blk = query[0]
 
@@ -218,7 +235,7 @@
         expos = jnp.exp2((scores - new_max) * factor)
         fading = jnp.exp2((highest - new_max) * factor)
         total = total * fading + jnp.sum(expos, axis=0, keepdims=True)
-        part = product(values[0, :, pl.ds(first, block)], expos.astype(jnp.bfloat16))
+        part = product(values[j // per, :, pl.ds(pl.multiple_of(j % per * block, block), block)], expos.astype(jnp.bfloat16))
         return new_max, total, acc * fading + part
 
     state = (
@@ -232,28 +249,32 @@
 
 
 def teacher_attend(fields):
-    channels, length = fields.shape[1:]
+    blocks, channels, rows = fields[0].shape
     heads = channels // HD
-    query, keys_t, values = fields.reshape(3, heads, HD, length)
-    block = math.gcd(length, 512)
+    length = blocks * rows
+    query, keys_t, values = fields
+    keys = keys_t.transpose(0, 2, 1).reshape(length, channels)
+    keys = keys.reshape(length, heads, HD).swapaxes(0, 1)
+    block = math.gcd(rows, 512)
+    per = rows // block
     pairs = heads * length * (length + block) // 2
-    attended = pl.pallas_call(
-        functools.partial(attend_kernel, block, HD ** (-0.5) * math.log2(math.e)),
+    tile = pl.BlockSpec((1, HD, block), lambda h, i: (i // per, h, i % per))
+    return pl.pallas_call(
+        functools.partial(attend_kernel, block, per, HD ** (-0.5) * math.log2(math.e)),
         grid=(heads, length // block),
         in_specs=[
-            pl.BlockSpec((1, HD, block), lambda h, i: (h, 0, i)),
+            tile,
             pl.BlockSpec((1, length, HD), lambda h, i: (h, 0, 0)),
-            pl.BlockSpec((1, HD, length), lambda h, i: (h, 0, 0)),
+            pl.BlockSpec((blocks, HD, rows), lambda h, i: (0, h, 0)),
         ],
-        out_specs=pl.BlockSpec((1, HD, block), lambda h, i: (h, 0, i)),
-        out_shape=jax.ShapeDtypeStruct((heads, HD, length), jnp.bfloat16),
+        out_specs=tile,
+        out_shape=jax.ShapeDtypeStruct((blocks, channels, rows), jnp.bfloat16),
         cost_estimate=pl.CostEstimate(
             flops=4 * HD * pairs, bytes_accessed=8 * channels * length, transcendentals=pairs
         ),
         compiler_params=pltpu.CompilerParams(vmem_limit_bytes=48 * 2**20),
         name="teacher_attend",
-    )(query, keys_t.swapaxes(1, 2), values)
-    return attended.reshape(channels, length)
+    )(query, keys, values)
 
 
 def attend_gathered(projected, teacher):
@@ -313,52 +334,63 @@
     return attended
 
 
+def swapped(value):
+    return lax.ppermute(value, "grp", [(0, 1), (1, 0)])
+
+
+def to_blocks(value):
+    return lax.all_to_all(value, "seq", split_axis=0, concat_axis=0, tiled=True)
+
+
 def body(seq_in, w_proj, w_out, filters):
     teacher = lax.axis_index("grp") == 0
     row_count = seq_in.shape[0]
+    half_rows = row_count // 2
     weights_in = w_proj[0]
     weights_out = w_out[0]
-    col_count = weights_in.shape[2]
+    feature_count, col_count = weights_in.shape[1:]
     seq_count = lax.axis_size("seq")
     chan_count = col_count // seq_count
     length = row_count * seq_count
     outer_len = 2 * length // 128
     tap_scale = length ** (-0.5)
-    block = weights_in
-    projected = lax.dot_general(
-        block,
-        lax.all_gather(seq_in, "head", axis=1, tiled=True),
-        (((1,), (1,)), ((), ())),
-        preferred_element_type=jnp.float32,
-    ).astype(jnp.bfloat16)
-    projected = projected.reshape(3, col_count, row_count)
+
+    own_rows = jnp.where(teacher, seq_in[:half_rows], seq_in[half_rows:])
+    own_rows = lax.all_gather(own_rows, "head", axis=1, tiled=True)
+    other_rows = swapped(own_rows)
+    features = jnp.concatenate(
+        [jnp.where(teacher, own_rows, other_rows), jnp.where(teacher, other_rows, own_rows)], axis=0
+    )
+    projected, fields = [], []
+    for which in range(3):
+        part = lax.dot_general(
+            weights_in[which],
+            features,
+            (((0,), (1,)), ((), ())),
+            preferred_element_type=jnp.float32,
+        ).astype(jnp.bfloat16)
+        projected.append(part)
+        fields.append(to_blocks(part.reshape(seq_count, chan_count, row_count)))
     by_heads = chan_count % HD == 0
-    spread = lax.all_to_all(
-        projected.reshape(3, seq_count, chan_count, row_count),
-        "seq",
-        split_axis=1,
-        concat_axis=3,
-        tiled=True,
-    )
-    fields_c = spread.reshape(3, chan_count, length)
     tables = dft_tables(length)
 
     def run_student(operands):
-        return student_forward(operands, tables, tap_scale)
+        fields, filters = operands
+        return student_forward((jnp.stack(fields), filters), tables, tap_scale)
 
     def run_teacher(operands):
         spec = jnp.zeros((chan_count * outer_len, 256), jnp.bfloat16)
         if by_heads:
             attended = teacher_attend(operands[0])
         else:
-            attended = jnp.zeros((chan_count, length), jnp.bfloat16)
+            attended = jnp.zeros((seq_count, chan_count, row_count), jnp.bfloat16)
         conv = jnp.zeros((chan_count, length // 128, 128), jnp.float32)
         return attended, conv, spec, spec
 
-    mixed, conv, spec_u, spec_h = lax.cond(teacher, run_teacher, run_student, (fields_c, filters))
-    mixed = lax.all_to_all(mixed, "seq", split_axis=1, concat_axis=0, tiled=True)
+    mixed, conv, spec_u, spec_h = lax.cond(teacher, run_teacher, run_student, (fields, filters))
+    mixed = to_blocks(mixed).reshape(col_count, row_count)
     if not by_heads:
-        mixed = jnp.where(teacher, attend_gathered(projected, teacher), mixed)
+        mixed = jnp.where(teacher, attend_gathered(jnp.stack(projected), teacher), mixed)
     y_own = lax.psum_scatter(
         lax.dot_general(
             weights_out, mixed, (((0,), (0,)), ((), ())), preferred_element_type=jnp.float32
@@ -367,57 +399,63 @@
         scatter_dimension=0,
         tiled=True,
     )
-    target = passed_along(y_own, "grp", 1)
-    diff = (y_own.astype(jnp.float32) - target.astype(jnp.float32)).astype(jnp.bfloat16)
-    portion = lax.all_gather(diff, "head", axis=0, tiled=True)
-    block = weights_out
-
-    def keep_sum(current):
-        return current
-
-    def grow_sum(current):
-        return jnp.dot(block, portion, preferred_element_type=jnp.float32)
-
-    d_gated = lax.cond(
-        teacher, keep_sum, grow_sum, jnp.zeros((col_count, row_count), jnp.float32)
-    ).astype(jnp.bfloat16)
-    d_spread = lax.all_to_all(
-        d_gated.reshape(seq_count, chan_count, row_count),
-        "seq",
-        split_axis=0,
-        concat_axis=2,
-        tiled=True,
-    ).reshape(chan_count, length)
+    y_first, y_last = y_own[:, :half_rows], y_own[:, half_rows:]
+    y_other = swapped(jnp.where(teacher, y_last, y_first)).astype(jnp.float32)
+    y_kept = jnp.where(teacher, y_first, y_last).astype(jnp.float32)
+    diff = jnp.where(teacher, y_other - y_kept, y_kept - y_other).astype(jnp.bfloat16)
+    portion_last = lax.all_gather(diff, "head", axis=0, tiled=True)
+    portion_first = passed_along(portion_last, "grp", 1)
+
+    def grown(portion):
+        return lax.cond(
+            teacher,
+            lambda current: jnp.zeros((col_count, half_rows), jnp.bfloat16),
+            lambda current: jnp.dot(
+                weights_out, current, preferred_element_type=jnp.float32
+            ).astype(jnp.bfloat16),
+            portion,
+        )
+
+    d_last = grown(portion_last)
+    d_gated = jnp.concatenate([grown(portion_first), d_last], axis=1)
+    d_spread = to_blocks(d_gated.reshape(seq_count, chan_count, row_count))
 
     def run_backward(operands):
-        return student_backward(operands, tables, tap_scale)
+        fields, *rest = operands
+        return student_backward((jnp.stack(fields), *rest), tables, tap_scale)
 
     def spare_backward(operands):
         return (
-            jnp.zeros((3, chan_count, length), jnp.bfloat16),
+            jnp.zeros((seq_count, 3, chan_count, row_count // 128, 128), jnp.bfloat16),
             jnp.zeros((chan_count, length), jnp.float32),
         )
 
     d_fields, d_taps = lax.cond(
-        teacher, spare_backward, run_backward, (fields_c, d_spread, conv, spec_u, spec_h)
-    )
-    d_rows = lax.all_to_all(d_fields, "seq", split_axis=2, concat_axis=1, tiled=True)
+        teacher, spare_backward, run_backward, (fields, d_spread, conv, spec_u, spec_h)
+    )
+    d_rows = to_blocks(d_fields)
+
+    def make_grad(operand):
+        rows = operand.reshape(seq_count, 3, chan_count, half_rows).swapaxes(0, 1)
+        return lax.dot_general(
+            weights_in,
+            rows.reshape(3, col_count, half_rows),
+            (((0, 2), (0, 1)), ((), ())),
+            preferred_element_type=jnp.float32,
+        ).astype(jnp.bfloat16)
 
     def skip_grad(operand):
-        return jnp.zeros((lax.axis_size("head") * col_count, row_count), jnp.float32)
-
-    def make_grad(operand):
-        return lax.dot_general(
-            weights_in, operand, (((0, 2), (0, 1)), ((), ())), preferred_element_type=jnp.float32
-        )
-
+        return jnp.zeros((feature_count, half_rows), jnp.bfloat16)
+
+    share = half_rows // 128
+    grad_first = lax.cond(teacher, skip_grad, make_grad, d_rows[:, :, :, :share])
+    from_student = passed_along(grad_first, "grp", -1)
+    grad_last = lax.cond(teacher, skip_grad, make_grad, d_rows[:, :, :, share:])
     d_input = lax.psum_scatter(
-        lax.cond(teacher, skip_grad, make_grad, d_rows).astype(jnp.bfloat16),
-        "head",
-        scatter_dimension=0,
-        tiled=True,
-    )
-    paired = jnp.where(teacher, y_own.T, d_input.T)[None]
+        jnp.where(teacher, from_student, grad_last), "head", scatter_dimension=0, tiled=True
+    )
+    d_first = passed_along(d_input, "grp", 1)
+    paired = jnp.where(teacher, y_own, jnp.concatenate([d_first, d_input], axis=1)).T[None]
     half_len = length // 2
     lower_taps = passed_along(d_taps[:, :half_len].astype(jnp.bfloat16), "grp", -1).astype(
         jnp.float32

time: 1020 us -> 876 us (0.86)
  waiting for transfers between devices: 681 us -> 522 us
  local copies, waits for them, and re-layouts: 116 us -> 63.5 us
  matrix products: 93 us -> 118 us
  other arithmetic: 10.3 us -> 31.3 us
  starting transfers between devices: 18 us -> 33.3 us
    all_gather x2, waiting for transfers between devices: 179 us -> 108 us  [the longest x1 55.4 us: body(): own_rows = lax.all_gather(own_rows, 'head', axis=1, tiled=True)]
    all_to_all x3 -> x5, waiting for transfers between devices: 297 us -> 246 us  [to_blocks(): return lax.all_to_all(value, 'seq', split_axis=0, concat_axis=0, tiled=True)]
    another operation x5 -> x0, local copies, waits for them, and re-layouts: 32.3 us -> none
    reduce_scatter x1, waiting for transfers between devices: 75.3 us -> 46.2 us  [body(): lax.psum_scatter(jnp.where(teacher, from_student, grad_last), 'head', sca...]
    dot_general x3 -> x7, matrix products: 78.4 us -> 104 us  [the longest x3 45.1 us: body(): lax.dot_general(weights_in[which], features, (((0,), (1,)), ((), ())), pr...]
    all_to_all x3 -> x0, local copies, waits for them, and re-layouts: 18.5 us -> none  [the longest x1 8.64 us: body(): lax.all_to_all(projected.reshape(3, seq_count, chan_count, row_count), 's...]
    select_n x0 -> x4, other arithmetic: none -> 14.2 us  [the longest x1 5.17 us: body(): jnp.where(teacher, own_rows, other_rows)]
    all_to_all x3 -> x5, starting transfers between devices: 15.2 us -> 23.3 us  [to_blocks(): return lax.all_to_all(value, 'seq', split_axis=0, concat_axis=0, tiled=True)]
  transfers between devices with their start and end apart: 9 -> 15, of which waited for: 9 -> 11; matrix products, arithmetic and copies ran while one was open for 1% -> 9% of each run, Pallas kernels for 0% -> 0%
where the time goes in v2:
time: 876 us; the launch traced here: 866 us
  waiting for transfers between devices  522 us (60%)
  matrix products  118 us (13%)
  local copies, waits for them, and re-layouts  63.5 us (7%)
  Pallas kernels  51.6 us (6%)
  starting transfers between devices  33.3 us (4%)
  other arithmetic  31.3 us (4%)
  blocking collectives  30 us (3%)
  between operations  14.4 us (2%)
    all_to_all x5, waiting for transfers between devices, to_blocks(): return lax.all_to_all(value, 'seq', split_axis=0, concat_axis=0, tiled=True)  246 us
    reduce_scatter x1, waiting for transfers between devices, body(): lax.psum_scatter(lax.dot_general(weights_out, mixed, (((0,), (0,)), ((),...  113 us
    all_gather x1, waiting for transfers between devices, body(): own_rows = lax.all_gather(own_rows, 'head', axis=1, tiled=True)  55.4 us
    all_gather x1, waiting for transfers between devices, body(): portion_last = lax.all_gather(diff, 'head', axis=0, tiled=True)  52.5 us
    reduce_scatter x1, waiting for transfers between devices, body(): lax.psum_scatter(jnp.where(teacher, from_student, grad_last), 'head', sca...  46.2 us
    dot_general x3, matrix products, body(): lax.dot_general(weights_in[which], features, (((0,), (1,)), ((), ())), pr...  45.1 us
    dot_general x2, matrix products, make_grad(): lax.dot_general(weights_in, rows.reshape(3, col_count, half_rows), (((0,...  40.4 us
    all_to_all x1, blocking collectives, to_blocks(): return lax.all_to_all(value, 'seq', split_axis=0, concat_axis=0, tiled=True)  30 us
  transfers between devices with their start and end apart: 15, of which 11 were waited for; matrix products, arithmetic and copies ran while one was open for 9% of the time, Pallas kernels for 0%

profile of v2, /device:TPU:1, one launch (start us, length us, event | category | flops | bytes accessed | tf_op | source)
XLA Modules:
  0.0 865.5 jit_solution(6977014853964771140)
XLA Ops:
  9.9 55.4 %all-gather.3.cloned.1.call-done = bf16[512,4096]{1,0:T(8,128)(2,1)} async-done(((bf16[512,1024]{1,0:T(8,128)(2,1)}), bf16[512,4096]{1,0:T(8,128)(2,1)}) %all-gather.3.cloned.1.call-update) | async-done | bytes 4194320 | tf_op jit(solution)/shard_map/all_gather | solution.py:359
  65.9 7.0 collective-permute-done
  72.9 5.2 broadcast_select_fusion.2
  78.1 15.0 %fusion.15 = bf16[1024,1024]{0,1:T(8,128)(2,1)} fusion(bf16[1,3,4096,1024]{3,2,1,0:T(8,128)(2,1)} %param.23, bf16[512,4096]{1,0:T(8,128)(2,1)} %get-tuple-element.162, bf16[512,4096]{1,0:T(8,128)(2,1)} %get-tuple-element.161), kind=kOutput, calls=%fused_computation.32 | convolution fusion | flops 8607760384 | bytes 18874368 | tf_op jit(solution)/shard_map/dot_general | solution.py:366
  93.1 4.3 all-to-all-start.1
  97.4 15.0 %fusion.18 = bf16[1024,1024]{0,1:T(8,128)(2,1)} fusion(bf16[1,3,4096,1024]{3,2,1,0:T(8,128)(2,1)} %param.23, bf16[512,4096]{1,0:T(8,128)(2,1)} %get-tuple-element.162, bf16[512,4096]{1,0:T(8,128)(2,1)} %get-tuple-element.161), kind=kOutput, calls=%fused_computation.33 | convolution fusion | flops 8607760384 | bytes 18874368 | tf_op jit(solution)/shard_map/dot_general | solution.py:366
  112.5 32.7 %all-to-all-done.1 = bf16[4,256,1024]{2,1,0:T(8,128)(2,1)S(1)} async-done(((bf16[4,256,1024]{2,1,0:T(8,128)(2,1)}), bf16[4,256,1024]{2,1,0:T(8,128)(2,1)S(1)}, u32[]{:S(2)}, u32[]{:S(2)}) %all-to-all-start.1) | async-done | bytes 2097184 | tf_op jit(solution)/shard_map/all_to_all | solution.py:342
  145.2 4.7 all-to-all-start.2
  149.9 15.1 %fusion.12 = bf16[1024,1024]{0,1:T(8,128)(2,1)} fusion(bf16[1,3,4096,1024]{3,2,1,0:T(8,128)(2,1)} %param.23, bf16[512,4096]{1,0:T(8,128)(2,1)} %get-tuple-element.162, bf16[512,4096]{1,0:T(8,128)(2,1)} %get-tuple-element.161), kind=kOutput, calls=%fused_computation.31 | convolution fusion | flops 8607760384 | bytes 18874368 | tf_op jit(solution)/shard_map/dot_general | solution.py:366
  165.0 32.6 %all-to-all-done.2 = bf16[4,256,1024]{2,1,0:T(8,128)(2,1)} async-done(((bf16[4,256,1024]{2,1,0:T(8,128)(2,1)}), bf16[4,256,1024]{2,1,0:T(8,128)(2,1)}, u32[]{:S(2)}, u32[]{:S(2)}) %all-to-all-start.2) | async-done | bytes 2097184 | tf_op jit(solution)/shard_map/all_to_all | solution.py:342
  197.6 4.5 all-to-all-start
  202.2 47.7 %all-to-all-done = bf16[4,256,1024]{2,1,0:T(8,128)(2,1)} async-done(((bf16[4,256,1024]{2,1,0:T(8,128)(2,1)}), bf16[4,256,1024]{2,1,0:T(8,128)(2,1)}, u32[]{:S(2)}, u32[]{:S(2)}) %all-to-all-start) | async-done | bytes 2097184 | tf_op jit(solution)/shard_map/all_to_all | solution.py:342
  249.9 39.3 %conditional.6 = (bf16[4,256,1024]{2,1,0:T(8,128)(2,1)}, f32[256,32,128]{2,1,0:T(8,128)}, bf16[16384,256]{1,0:T(8,128)(2,1)}, bf16[16384,256]{1,0:T(8,128)(2,1)}) conditional(s32[]{:T(128)} %convert_element_type.57, (bf16[4,256,1024]{2,1,0:T(8,128)(2,1)}, bf16[4,256,1024]{2,1,0:T(8,128)(2,1)S(1)}, bf16[4,256,1024]{2,1,0:T(8,128)(2,1)}, ...), branch_computations={%region_0.1_spmd, %region_1.2_spmd} | conditional | flops 9663676416 | bytes 85246016 | solution.py:390
  255.0 3.4 pad_maximum_fusion.fields
  259.4 2.8 copy.40
  262.2 24.7 %student_forward.1 = (bf16[4,256,8,128]{3,2,1,0:T(8,128)(2,1)S(1)}, f32[256,32,128]{2,1,0:T(8,128)}, bf16[16384,256]{1,0:T(8,128)(2,1)}, bf16[16384,256]{1,0:T(8,128)(2,1)}) custom-call(bf16[3,4,256,8,128]{4,3,2,1,0:T(8,128)(2,1)} %pad_maximum_fusion.fields, f32[256,32,128]{2,1,0:T(8,128)} %bitcast.112, bf16[1024,256]{1,0:T(8,128)(2,1)S(1)} %get-tuple-element.86.first, ...), custom_call_target="tpu_custom_call" | custom-call | flops 9216000000 | bytes 30720000 | tf_op jit(solution)/shard_map/cond/branch_0_fun/student_forward/pallas_call | solution.py:179
  289.2 30.0 %all_to_all.30 = bf16[4,256,1024]{2,1,0:T(8,128)(2,1)S(1)} all-to-all(bf16[4,256,1024]{2,1,0:T(8,128)(2,1)} %get-tuple-element.130), channel_id=1, replica_groups=mesh['grp'=2,'head'=4,'seq'=4] {'seq'}, dimensions={0} | all-to-all | bytes 4194304 | tf_op jit(solution)/shard_map/all_to_all | solution.py:342
  319.1 14.6 %convert_bitcast_fusion = bf16[4096,1024]{0,1:T(8,128)(2,1)} fusion(bf16[1024,1024]{1,0:T(8,128)(2,1)S(1)} %bitcast.119, bf16[1,1024,4096]{2,1,0:T(8,128)(2,1)} %param.24), kind=kOutput, calls=%fused_computation.15 | convolution fusion | flops 8594128896 | bytes 18874368 | tf_op jit(solution)/shard_map/dot_general | solution.py:395
  333.8 113.2 %reduce-scatter.3.cloned.1.call-done = bf16[1024,1024]{0,1:T(8,128)(2,1)} async-done(((bf16[4096,1024]{0,1:T(8,128)(2,1)}), bf16[1024,1024]{0,1:T(8,128)(2,1)}) %reduce-scatter.3.cloned.1.call-update) | async-done | bytes 2097168 | tf_op jit(solution)/shard_map/reduce_scatter | solution.py:394
  453.6 52.5 %all-gather.5.cloned.1.call-done = bf16[4096,512]{0,1:T(8,128)(2,1)} async-done(((bf16[1024,512]{0,1:T(8,128)(2,1)}), bf16[4096,512]{0,1:T(8,128)(2,1)}) %all-gather.5.cloned.1.call-update) | async-done | bytes 4194320 | tf_op jit(solution)/shard_map/all_gather | solution.py:406
  507.5 9.1 %conditional.8 = (bf16[1024,512]{1,0:T(8,128)(2,1)S(1)}) conditional(s32[]{:T(128)} %convert_element_type.57, (bf16[1024,4096]{1,0:T(8,128)(2,1)}, bf16[4096,512]{0,1:T(8,128)(2,1)}) %tuple.97, () %tuple.53), branch_computations={%region_5.6_spmd, %region_6.7_spmd} | conditional | flops 4295491584 | bytes 13631496 | solution.py:410
  507.5 9.1 %convolution_convert_fusion.1 = bf16[1024,512]{1,0:T(8,128)(2,1)S(1)} fusion(bf16[1024,4096]{1,0:T(8,128)(2,1)} %get-tuple-element.101, bf16[4096,512]{0,1:T(8,128)(2,1)} %get-tuple-element.155), kind=kOutput, calls=%fused_computation.3 | convolution fusion | flops 4295491584 | bytes 13631488 | tf_op jit(solution)/shard_map/cond/branch_0_fun/dot_general | solution.py:413
  516.6 9.3 %conditional.7 = (bf16[1024,512]{1,0:T(8,128)(2,1)S(1)}) conditional(s32[]{:T(128)} %convert_element_type.57, (bf16[1024,4096]{1,0:T(8,128)(2,1)}, bf16[4096,512]{0,1:T(8,128)(2,1)}) %tuple.98, () %tuple.51), branch_computations={%region_3.4_spmd, %region_4.5_spmd} | conditional | flops 4295491584 | bytes 13631496 | solution.py:410
  516.8 9.1 %convolution_convert_fusion = bf16[1024,512]{1,0:T(8,128)(2,1)S(1)} fusion(bf16[1024,4096]{1,0:T(8,128)(2,1)} %get-tuple-element.99, bf16[4096,512]{0,1:T(8,128)(2,1)} %get-tuple-element.153), kind=kOutput, calls=%fused_computation.2 | convolution fusion | flops 4295491584 | bytes 13631488 | tf_op jit(solution)/shard_map/cond/branch_0_fun/dot_general | solution.py:413
  526.9 3.0 pad_maximum_fusion.6
  529.9 4.6 all-to-all-start.4
  534.5 39.2 %all-to-all-done.4 = bf16[4,256,1024]{2,1,0:T(8,128)(2,1)} async-done(((bf16[4,256,1024]{2,1,0:T(8,128)(2,1)}), bf16[4,256,1024]{2,1,0:T(8,128)(2,1)}, u32[]{:S(2)}, u32[]{:S(2)}) %all-to-all-start.4) | async-done | bytes 2097184 | tf_op jit(solution)/shard_map/all_to_all | solution.py:342
  573.7 46.1 %conditional.9 = (bf16[4,3,256,8,128]{4,3,2,1,0:T(8,128)(2,1)S(1)}, f32[256,4096]{1,0:T(8,128)}) conditional(s32[]{:T(128)} %convert_element_type.57, (bf16[4,256,1024]{2,1,0:T(8,128)(2,1)}, bf16[4,256,1024]{2,1,0:T(8,128)(2,1)S(1)}, bf16[4,256,1024]{2,1,0:T(8,128)(2,1)}, bf16[4,256,1024]{2,1,0:T(8,128)(2,1)}, f32[256,32,128]{2,1,0:T(8,128)}, ...), branch_computations={%region_7.8_spmd, %region_8.9_spmd} | conditional | flops 9222291456 | bytes 85246000 | solution.py:433
  578.8 3.1 pad_maximum_fusion.1.fields
  584.7 26.9 %student_backward.1 = (bf16[4,3,256,8,128]{4,3,2,1,0:T(8,128)(2,1)S(1)}, f32[256,32,128]{2,1,0:T(8,128)}) custom-call(bf16[3,4,256,8,128]{4,3,2,1,0:T(8,128)(2,1)} %pad_maximum_fusion.1.fields, bf16[4,256,8,128]{3,2,1,0:T(8,128)(2,1)S(1)} %bitcast.99, f32[256,32,128]{2,1,0:T(8,128)S(1)} %copy-done.9, bf16[16384,256]{1,0:T(8,128)(2,1)} %get-tuple-element.108.spec_u, ...), custom_call_target="tpu_custom_call" | custom-call | flops 9216000000 | bytes 30720000 | tf_op jit(solution)/shard_map/cond/branch_0_fun/student_backward/pallas_call | solution.py:206
  611.6 8.0 copy.49
  619.8 2.7 copy-done.5
  622.5 5.3 all-to-all-start.5
  627.8 93.5 %all-to-all-done.5 = bf16[4,3,256,8,128]{4,3,2,1,0:T(8,128)(2,1)} async-done(((bf16[4,3,256,8,128]{4,3,2,1,0:T(8,128)(2,1)}), bf16[4,3,256,8,128]{4,3,2,1,0:T(8,128)(2,1)}, u32[]{:S(2)}, u32[]{:S(2)}) %all-to-all-start.5) | async-done | bytes 6291488 | tf_op jit(solution)/shard_map/all_to_all | solution.py:342
  721.3 3.2 copy.29
  727.2 24.6 %conditional.10 = (bf16[4096,512]{1,0:T(8,128)(2,1)}) conditional(s32[]{:T(128)} %convert_element_type.57, (bf16[4,3,256,8,128]{4,3,2,0,1:T(8,128)(2,1)S(1)}, bf16[3,4096,1024]{2,1,0:T(8,128)(2,1)}) %tuple.95, () %tuple.57), branch_computations={%region_9.10_spmd, %region_10.11_spmd} | conditional | flops 12886999040 | bytes 45088776 | solution.py:451
  728.3 3.3 reshape.57
  731.6 20.2 %bitcast_convert_fusion = bf16[4096,512]{1,0:T(8,128)(2,1)} fusion(bf16[3,4096,1024]{2,1,0:T(8,128)(2,1)} %get-tuple-element.118, bf16[3,1024,512]{2,1,0:T(8,128)(2,1)} %bitcast.114), kind=kOutput, calls=%fused_computation.6 | convolution fusion | flops 12886999040 | bytes 32505856 | tf_op jit(solution)/shard_map/cond/branch_0_fun/dot_general | solution.py:440
  751.8 6.4 copy.30
  758.2 3.3 collective-permute-start.3
  761.6 34.7 %conditional.11 = (bf16[4096,512]{0,1:T(8,128)(2,1)}) conditional(s32[]{:T(128)} %convert_element_type.57, (bf16[4,3,256,8,128]{4,3,2,0,1:T(8,128)(2,1)}, bf16[3,4096,1024]{2,1,0:T(8,128)(2,1)}) %tuple.96, () %tuple.58), branch_computations={%region_11.12_spmd, %region_12.13_spmd} | conditional | flops 12886999040 | bytes 53477384 | solution.py:453
  761.8 4.5 slice.29
  766.3 3.3 reshape.59
  769.6 20.2 %bitcast_convert_fusion.1 = bf16[4096,512]{1,0:T(8,128)(2,1)} fusion(bf16[3,4096,1024]{2,1,0:T(8,128)(2,1)} %get-tuple-element.120, bf16[3,1024,512]{2,1,0:T(8,128)(2,1)} %bitcast.115), kind=kOutput, calls=%fused_computation.7 | convolution fusion | flops 12886999040 | bytes 32505856 | tf_op jit(solution)/shard_map/cond/branch_0_fun/dot_general | solution.py:440
  789.8 6.4 copy.35
  796.2 4.6 broadcast_select_fusion
  805.1 46.2 %reduce-scatter.5.cloned.1.call-done = bf16[1024,512]{0,1:T(8,128)(2,1)} async-done(((bf16[4096,512]{0,1:T(8,128)(2,1)}), bf16[1024,512]{0,1:T(8,128)(2,1)}) %reduce-scatter.5.cloned.1.call-update) | async-done | bytes 1048592 | tf_op jit(solution)/shard_map/reduce_scatter | solution.py:454
  852.7 3.5 slice_select_fusion
  (65 shorter events, 40.3 us)
Async XLA Ops:
  7.2 58.1 %all-gather.3.cloned.1.call-start = ((), (), s32[]{:S(2)}) async-start(), calls=%async_computation.8 | async-start | bytes 5242880 | tf_op jit(solution)/shard_map/all_gather | solution.py:359
  65.2 7.7 collective-permute-start
  93.1 52.1 %all-to-all-start.1 = ((bf16[4,256,1024]{2,1,0:T(8,128)(2,1)}), bf16[4,256,1024]{2,1,0:T(8,128)(2,1)S(1)}, u32[]{:S(2)}, u32[]{:S(2)}) async-start(bf16[4,256,1024]{2,1,0:T(8,128)(2,1)} %bitcast.118), calls=%async_computation.1 | async-start | bytes 4194304 | tf_op jit(solution)/shard_map/all_to_all | solution.py:342
  145.2 104.7 %copy-start = (bf16[4,256,1024]{2,1,0:T(8,128)(2,1)}, bf16[4,256,1024]{2,1,0:T(8,128)(2,1)S(1)}, u32[]{:S(2)}) copy-start(bf16[4,256,1024]{2,1,0:T(8,128)(2,1)S(1)} %all-to-all-done.1) | copy-start | bytes 6291460
  145.2 52.4 %all-to-all-start.2 = ((bf16[4,256,1024]{2,1,0:T(8,128)(2,1)}), bf16[4,256,1024]{2,1,0:T(8,128)(2,1)}, u32[]{:S(2)}, u32[]{:S(2)}) async-start(bf16[4,256,1024]{2,1,0:T(8,128)(2,1)} %bitcast.117), calls=%async_computation.2 | async-start | bytes 4194304 | tf_op jit(solution)/shard_map/all_to_all | solution.py:342
  165.0 84.9 %copy-start.10 = (bf16[1024,256]{1,0:T(8,128)(2,1)S(1)}, bf16[1024,256]{1,0:T(8,128)(2,1)}, u32[]{:S(2)}) copy-start(bf16[1024,256]{1,0:T(8,128)(2,1)} %constant.36.clone) | copy-start | bytes 1572868
  165.0 84.9 %copy-start.12 = (bf16[256,256]{1,0:T(8,128)(2,1)S(1)}, bf16[256,256]{1,0:T(8,128)(2,1)}, u32[]{:S(2)}) copy-start(bf16[256,256]{1,0:T(8,128)(2,1)} %constant.38.clone) | copy-start | bytes 393220
  165.0 84.9 %copy-start.13 = (bf16[256,256]{1,0:T(8,128)(2,1)S(1)}, bf16[256,256]{1,0:T(8,128)(2,1)}, u32[]{:S(2)}) copy-start(bf16[256,256]{1,0:T(8,128)(2,1)} %constant.37.clone) | copy-start | bytes 393220
  165.0 84.9 %copy-start.14 = (f32[64,128]{1,0:T(8,128)S(1)}, f32[64,128]{1,0:T(8,128)}, u32[]{:S(2)}) copy-start(f32[64,128]{1,0:T(8,128)} %constant.41.clone) | copy-start | bytes 98308
  165.0 84.9 %copy-start.15 = (f32[64,128]{1,0:T(8,128)S(1)}, f32[64,128]{1,0:T(8,128)}, u32[]{:S(2)}) copy-start(f32[64,128]{1,0:T(8,128)} %constant.40.clone) | copy-start | bytes 98308
  165.0 84.9 %copy-start.16 = (bf16[64,256]{1,0:T(8,128)(2,1)S(1)}, bf16[64,256]{1,0:T(8,128)(2,1)}, u32[]{:S(2)}) copy-start(bf16[64,256]{1,0:T(8,128)(2,1)} %constant.39.clone) | copy-start | bytes 98308
  197.6 52.2 %all-to-all-start = ((bf16[4,256,1024]{2,1,0:T(8,128)(2,1)}), bf16[4,256,1024]{2,1,0:T(8,128)(2,1)}, u32[]{:S(2)}, u32[]{:S(2)}) async-start(bf16[4,256,1024]{2,1,0:T(8,128)(2,1)} %bitcast.116), calls=%async_computation | async-start | bytes 4194304 | tf_op jit(solution)/shard_map/all_to_all | solution.py:342
  202.1 244.9 %reduce-scatter.3.cloned.1.call-start = ((), (), s32[]{:S(2)}) async-start(), calls=%async_computation.9 | async-start | bytes 10485760 | tf_op jit(solution)/shard_map/reduce_scatter | solution.py:394
  255.0 4.4 copy-start.6
  333.7 172.4 %all-gather.5.cloned.1.call-start = ((), (), s32[]{:S(2)}) async-start(), calls=%async_computation.10 | async-start | bytes 5242880 | tf_op jit(solution)/shard_map/all_gather | solution.py:406
  447.0 4.9 copy-start.3
  448.8 3.1 collective-permute-start.1
  506.2 10.4 %collective-permute-start.2 = (bf16[4096,512]{0,1:T(8,128)(2,1)}, bf16[4096,512]{0,1:T(8,128)(2,1)}, u32[]{:S(2)}, u32[]{:S(2)}) collective-permute-start(bf16[4096,512]{0,1:T(8,128)(2,1)} %all-gather.5.cloned.1.call-done), channel_id=1, source_target_pairs={{0,16},{1,17},{2,18},{3,19},{4,20},{5,21},{6,22},{7,23},{8,24},{9,... | collective-permute-start | bytes 12582920 | tf_op jit(solution)/shard_map/ppermute | solution.py:20
  525.9 1.0 copy-start.8
  526.9 46.8 %copy-start.1 = (bf16[4,256,1024]{2,1,0:T(8,128)(2,1)S(1)}, bf16[4,256,1024]{2,1,0:T(8,128)(2,1)}, u32[]{:S(2)}) copy-start(bf16[4,256,1024]{2,1,0:T(8,128)(2,1)} %copy-done) | copy-start | bytes 6291460
  529.9 43.8 %copy-start.11 = (bf16[1024,256]{1,0:T(8,128)(2,1)S(1)}, bf16[1024,256]{1,0:T(8,128)(2,1)}, u32[]{:S(2)}) copy-start(bf16[1024,256]{1,0:T(8,128)(2,1)} %constant.36.clone) | copy-start | bytes 1572868
  529.9 43.8 %all-to-all-start.4 = ((bf16[4,256,1024]{2,1,0:T(8,128)(2,1)}), bf16[4,256,1024]{2,1,0:T(8,128)(2,1)}, u32[]{:S(2)}, u32[]{:S(2)}) async-start(bf16[4,256,1024]{2,1,0:T(8,128)(2,1)} %bitcast.103), calls=%async_computation.5 | async-start | bytes 4194304 | tf_op jit(solution)/shard_map/all_to_all | solution.py:342
  581.9 2.8 copy-start.9
  619.8 2.7 copy-start.5
  622.5 98.8 %all-to-all-start.5 = ((bf16[4,3,256,8,128]{4,3,2,1,0:T(8,128)(2,1)}), bf16[4,3,256,8,128]{4,3,2,1,0:T(8,128)(2,1)}, u32[]{:S(2)}, u32[]{:S(2)}) async-start(bf16[4,3,256,8,128]{4,3,2,1,0:T(8,128)(2,1)} %copy-done.5), calls=%async_computation.6 | async-start | bytes 12582912 | tf_op jit(solution)/shard_map/all_to_all | solution.py:342
  627.8 223.5 %reduce-scatter.5.cloned.1.call-start = ((), (), s32[]{:S(2)}) async-start(), calls=%async_computation.11 | async-start | bytes 5242880 | tf_op jit(solution)/shard_map/reduce_scatter | solution.py:454
  724.5 2.7 copy-start.2
  758.2 38.0 %collective-permute-start.3 = (bf16[4096,512]{0,1:T(8,128)(2,1)}, bf16[4096,512]{0,1:T(8,128)(2,1)}, u32[]{:S(2)}, u32[]{:S(2)}) collective-permute-start(bf16[4096,512]{0,1:T(8,128)(2,1)} %copy.30), channel_id=1, source_target_pairs={{16,0},{17,1},{18,2},{19,3},{20,4},{21,5},{22,6},{23,7},{24,8},{25... | collective-permute-start | bytes 12582920 | tf_op jit(solution)/shard_map/ppermute | solution.py:20
  800.9 55.4 %copy-start.4 = (bf16[1024,1024]{0,1:T(8,128)(2,1)S(1)}, bf16[1024,1024]{0,1:T(8,128)(2,1)}, u32[]{:S(2)}) copy-start(bf16[1024,1024]{0,1:T(8,128)(2,1)} %reduce-scatter.3.cloned.1.call-done) | copy-start | bytes 6291460
  802.8 49.9 %collective-permute-start.5 = (bf16[256,2048]{1,0:T(8,128)(2,1)S(1)}, bf16[256,2048]{1,0:T(8,128)(2,1)}, u32[]{:S(2)}, u32[]{:S(2)}) collective-permute-start(bf16[256,2048]{1,0:T(8,128)(2,1)S(1)} %slice.77), channel_id=1, source_target_pairs={{16,0},{17,1},{18,2},{19,3},{20,4},{21,5},{22,6},{23,7},{24,8},{25... | collective-permute-start | bytes 3145736 | tf_op jit(solution)/shard_map/ppermute | solution.py:20
  851.3 5.0 copy-start.7
  851.3 5.0 collective-permute-start.4
Sparse Core Ops, SparseCore 0:
  10.4 54.7 all-gather.2
  333.9 113.1 reduce-scatter.2
  453.7 52.3 all-gather.4
  801.0 50.2 reduce-scatter.4

commit v3 on v2

--- a/solution.py
+++ b/solution.py
@@ -355,6 +355,9 @@
     outer_len = 2 * length // 128
     tap_scale = length ** (-0.5)
 
+    student_in = passed_along(weights_in, "grp", -1)
+    student_out = passed_along(weights_out, "grp", -1)
+
     own_rows = jnp.where(teacher, seq_in[:half_rows], seq_in[half_rows:])
     own_rows = lax.all_gather(own_rows, "head", axis=1, tiled=True)
     other_rows = swapped(own_rows)
@@ -403,57 +406,57 @@
     y_other = swapped(jnp.where(teacher, y_last, y_first)).astype(jnp.float32)
     y_kept = jnp.where(teacher, y_first, y_last).astype(jnp.float32)
     diff = jnp.where(teacher, y_other - y_kept, y_kept - y_other).astype(jnp.bfloat16)
-    portion_last = lax.all_gather(diff, "head", axis=0, tiled=True)
-    portion_first = passed_along(portion_last, "grp", 1)
-
-    def grown(portion):
-        return lax.cond(
-            teacher,
-            lambda current: jnp.zeros((col_count, half_rows), jnp.bfloat16),
-            lambda current: jnp.dot(
-                weights_out, current, preferred_element_type=jnp.float32
-            ).astype(jnp.bfloat16),
-            portion,
-        )
-
-    d_last = grown(portion_last)
-    d_gated = jnp.concatenate([grown(portion_first), d_last], axis=1)
-    d_spread = to_blocks(d_gated.reshape(seq_count, chan_count, row_count))
+    portion = lax.all_gather(diff, "head", axis=0, tiled=True)
+
+    def grown(weights, current):
+        return jnp.dot(weights, current, preferred_element_type=jnp.float32).astype(jnp.bfloat16)
+
+    d_gated = lax.cond(
+        teacher,
+        lambda theirs, own, current: grown(theirs, current),
+        lambda theirs, own, current: grown(own, current),
+        student_out,
+        weights_out,
+        portion,
+    )
+    d_last = to_blocks(d_gated.reshape(seq_count, chan_count, half_rows))
+    d_first = passed_along(d_last, "grp", 1)
+    d_spread = jnp.concatenate([d_first, d_last], axis=2)
+
+    share = half_rows // 128
+    half_shape = (seq_count, 3, chan_count, half_rows)
 
     def run_backward(operands):
         fields, *rest = operands
-        return student_backward((jnp.stack(fields), *rest), tables, tap_scale)
+        d_fields, d_taps = student_backward((jnp.stack(fields), *rest), tables, tap_scale)
+        d_fields = d_fields.reshape(seq_count, 3, chan_count, 2 * share, 128)
+        first = d_fields[:, :, :, :share].reshape(half_shape)
+        return first, d_fields[:, :, :, share:].reshape(half_shape), d_taps
 
     def spare_backward(operands):
-        return (
-            jnp.zeros((seq_count, 3, chan_count, row_count // 128, 128), jnp.bfloat16),
-            jnp.zeros((chan_count, length), jnp.float32),
-        )
-
-    d_fields, d_taps = lax.cond(
+        spare = jnp.zeros(half_shape, jnp.bfloat16)
+        return spare, spare, jnp.zeros((chan_count, length), jnp.float32)
+
+    d_first, d_last, d_taps = lax.cond(
         teacher, spare_backward, run_backward, (fields, d_spread, conv, spec_u, spec_h)
     )
-    d_rows = to_blocks(d_fields)
-
-    def make_grad(operand):
-        rows = operand.reshape(seq_count, 3, chan_count, half_rows).swapaxes(0, 1)
+    d_rows = to_blocks(jnp.where(teacher, passed_along(d_first, "grp", -1), d_last))
+    d_rows = d_rows.swapaxes(0, 1).reshape(3, col_count, half_rows)
+
+    def make_grad(weights, rows):
         return lax.dot_general(
-            weights_in,
-            rows.reshape(3, col_count, half_rows),
-            (((0, 2), (0, 1)), ((), ())),
-            preferred_element_type=jnp.float32,
+            weights, rows, (((0, 2), (0, 1)), ((), ())), preferred_element_type=jnp.float32
         ).astype(jnp.bfloat16)
 
-    def skip_grad(operand):
-        return jnp.zeros((feature_count, half_rows), jnp.bfloat16)
-
-    share = half_rows // 128
-    grad_first = lax.cond(teacher, skip_grad, make_grad, d_rows[:, :, :, :share])
-    from_student = passed_along(grad_first, "grp", -1)
-    grad_last = lax.cond(teacher, skip_grad, make_grad, d_rows[:, :, :, share:])
-    d_input = lax.psum_scatter(
-        jnp.where(teacher, from_student, grad_last), "head", scatter_dimension=0, tiled=True
-    )
+    grad = lax.cond(
+        teacher,
+        lambda theirs, own, rows: make_grad(theirs, rows),
+        lambda theirs, own, rows: make_grad(own, rows),
+        student_in,
+        weights_in,
+        d_rows,
+    )
+    d_input = lax.psum_scatter(grad, "head", scatter_dimension=0, tiled=True)
     d_first = passed_along(d_input, "grp", 1)
     paired = jnp.where(teacher, y_own, jnp.concatenate([d_first, d_input], axis=1)).T[None]
     half_len = length // 2

time: 876 us -> 803 us (0.917)
  waiting for transfers between devices: 522 us -> 354 us
  blocking collectives: 30 us -> 131 us
  starting transfers between devices: 33.3 us -> 70.7 us
  matrix products: 118 us -> 88.2 us
    all_to_all x5 -> x3, waiting for transfers between devices: 246 us -> 113 us  [to_blocks(): return lax.all_to_all(value, 'seq', split_axis=0, concat_axis=0, tiled=True)]
    all_to_all x1 -> x3, blocking collectives: 30 us -> 131 us  [to_blocks(): return lax.all_to_all(value, 'seq', split_axis=0, concat_axis=0, tiled=True)]
    ppermute x4 -> x6, starting transfers between devices: 8.37 us -> 55.4 us  [passed_along(): return lax.ppermute(value, axis, pairs)]
    reduce_scatter x1, waiting for transfers between devices: 113 us -> 68.7 us  [body(): lax.psum_scatter(lax.dot_general(weights_out, mixed, (((0,), (0,)), ((),...]
    dot_general x4 -> x2, matrix products: 58.6 us -> 28.5 us  [the longest x1 19.4 us: make_grad(): lax.dot_general(weights, rows, (((0, 2), (0, 1)), ((), ())), preferred_el...]
    cond x16 -> x15, local copies, waits for them, and re-layouts: 40.8 us -> 24.1 us
    all_to_all x5 -> x3, starting transfers between devices: 23.3 us -> 13.7 us  [to_blocks(): return lax.all_to_all(value, 'seq', split_axis=0, concat_axis=0, tiled=True)]
    ppermute x4 -> x6, waiting for transfers between devices: 0.01 us -> 9.22 us  [passed_along(): return lax.ppermute(value, axis, pairs)]
  transfers between devices with their start and end apart: 15 -> 15, of which waited for: 11 -> 11; matrix products, arithmetic and copies ran while one was open for 9% -> 11% of each run, Pallas kernels for 0% -> 3%
where the time goes in v3:
time: 803 us; the launch traced here: 793 us
  waiting for transfers between devices  354 us (44%)
  blocking collectives  131 us (16%)
  matrix products  88.2 us (11%)
  starting transfers between devices  70.7 us (9%)
  local copies, waits for them, and re-layouts  55.4 us (7%)
  Pallas kernels  51.7 us (6%)
  other arithmetic  26.6 us (3%)
  between operations  14.2 us (2%)
    all_to_all x3, blocking collectives, to_blocks(): return lax.all_to_all(value, 'seq', split_axis=0, concat_axis=0, tiled=True)  131 us
    all_to_all x3, waiting for transfers between devices, to_blocks(): return lax.all_to_all(value, 'seq', split_axis=0, concat_axis=0, tiled=True)  113 us
    reduce_scatter x1, waiting for transfers between devices, body(): lax.psum_scatter(lax.dot_general(weights_out, mixed, (((0,), (0,)), ((),...  68.7 us
    all_gather x1, waiting for transfers between devices, body(): own_rows = lax.all_gather(own_rows, 'head', axis=1, tiled=True)  55.4 us
    ppermute x6, starting transfers between devices, passed_along(): return lax.ppermute(value, axis, pairs)  55.4 us
    all_gather x1, waiting for transfers between devices, body(): portion = lax.all_gather(diff, 'head', axis=0, tiled=True)  52.5 us
    reduce_scatter x1, waiting for transfers between devices, body(): d_input = lax.psum_scatter(grad, 'head', scatter_dimension=0, tiled=True)  46 us
    dot_general x3, matrix products, body(): lax.dot_general(weights_in[which], features, (((0,), (1,)), ((), ())), pr...  45.2 us
  transfers between devices with their start and end apart: 15, of which 11 were waited for; matrix products, arithmetic and copies ran while one was open for 11% of the time, Pallas kernels for 3%

profile of v3, /device:TPU:1, one launch (start us, length us, event | category | flops | bytes accessed | tf_op | source)
XLA Modules:
  0.0 792.7 jit_solution(8760728498858027764)
XLA Ops:
  7.2 2.6 slice_select_fusion.1
  9.9 55.4 %all-gather.3.cloned.1.call-done = bf16[512,4096]{1,0:T(8,128)(2,1)} async-done(((bf16[512,1024]{1,0:T(8,128)(2,1)}), bf16[512,4096]{1,0:T(8,128)(2,1)}) %all-gather.3.cloned.1.call-update) | async-done | bytes 4194320 | tf_op jit(solution)/shard_map/all_gather | solution.py:362
  65.9 7.0 collective-permute-done
  72.9 5.3 broadcast_select_fusion.1
  78.2 15.1 %fusion.18 = bf16[1024,1024]{0,1:T(8,128)(2,1)} fusion(bf16[1,3,4096,1024]{3,2,1,0:T(8,128)(2,1)} %param.19, bf16[512,4096]{1,0:T(8,128)(2,1)} %get-tuple-element.150, bf16[512,4096]{1,0:T(8,128)(2,1)} %get-tuple-element.149), kind=kOutput, calls=%fused_computation.31 | convolution fusion | flops 8607760384 | bytes 18874368 | tf_op jit(solution)/shard_map/dot_general | solution.py:369
  93.2 4.3 all-to-all-start.2
  97.5 15.1 %fusion.15 = bf16[1024,1024]{0,1:T(8,128)(2,1)} fusion(bf16[1,3,4096,1024]{3,2,1,0:T(8,128)(2,1)} %param.19, bf16[512,4096]{1,0:T(8,128)(2,1)} %get-tuple-element.150, bf16[512,4096]{1,0:T(8,128)(2,1)} %get-tuple-element.149), kind=kOutput, calls=%fused_computation.30 | convolution fusion | flops 8607760384 | bytes 18874368 | tf_op jit(solution)/shard_map/dot_general | solution.py:369
  112.6 32.7 %all-to-all-done.2 = bf16[4,256,1024]{2,1,0:T(8,128)(2,1)S(1)} async-done(((bf16[4,256,1024]{2,1,0:T(8,128)(2,1)}), bf16[4,256,1024]{2,1,0:T(8,128)(2,1)S(1)}, u32[]{:S(2)}, u32[]{:S(2)}) %all-to-all-start.2) | async-done | bytes 2097184 | tf_op jit(solution)/shard_map/all_to_all | solution.py:342
  145.3 4.9 all-to-all-start.1
  150.2 15.1 %fusion.12 = bf16[1024,1024]{0,1:T(8,128)(2,1)} fusion(bf16[1,3,4096,1024]{3,2,1,0:T(8,128)(2,1)} %param.19, bf16[512,4096]{1,0:T(8,128)(2,1)} %get-tuple-element.150, bf16[512,4096]{1,0:T(8,128)(2,1)} %get-tuple-element.149), kind=kOutput, calls=%fused_computation.29 | convolution fusion | flops 8607760384 | bytes 18874368 | tf_op jit(solution)/shard_map/dot_general | solution.py:369
  165.3 32.6 %all-to-all-done.1 = bf16[4,256,1024]{2,1,0:T(8,128)(2,1)} async-done(((bf16[4,256,1024]{2,1,0:T(8,128)(2,1)}), bf16[4,256,1024]{2,1,0:T(8,128)(2,1)}, u32[]{:S(2)}, u32[]{:S(2)}) %all-to-all-start.1) | async-done | bytes 2097184 | tf_op jit(solution)/shard_map/all_to_all | solution.py:342
  198.0 4.5 all-to-all-start
  202.5 47.7 %all-to-all-done = bf16[4,256,1024]{2,1,0:T(8,128)(2,1)} async-done(((bf16[4,256,1024]{2,1,0:T(8,128)(2,1)}), bf16[4,256,1024]{2,1,0:T(8,128)(2,1)}, u32[]{:S(2)}, u32[]{:S(2)}) %all-to-all-start) | async-done | bytes 2097184 | tf_op jit(solution)/shard_map/all_to_all | solution.py:342
  250.2 39.1 %conditional.12 = (bf16[4,256,1024]{2,1,0:T(8,128)(2,1)}, f32[256,32,128]{2,1,0:T(8,128)}, bf16[16384,256]{1,0:T(8,128)(2,1)}, bf16[16384,256]{1,0:T(8,128)(2,1)}) conditional(s32[]{:T(128)} %convert_element_type.53, (bf16[4,256,1024]{2,1,0:T(8,128)(2,1)}, bf16[4,256,1024]{2,1,0:T(8,128)(2,1)}, bf16[4,256,1024]{2,1,0:T(8,128)(2,1)S(1)}, ...), branch_computations={%region_0.1_spmd, %region_1.2_spmd} | conditional | flops 9663676416 | bytes 85246016 | solution.py:393
  252.4 2.2 copy.26
  255.3 3.4 pad_maximum_fusion.fields
  259.7 2.7 copy.28
  262.4 24.7 %student_forward.1 = (bf16[4,256,8,128]{3,2,1,0:T(8,128)(2,1)S(1)}, f32[256,32,128]{2,1,0:T(8,128)}, bf16[16384,256]{1,0:T(8,128)(2,1)}, bf16[16384,256]{1,0:T(8,128)(2,1)}) custom-call(bf16[3,4,256,8,128]{4,3,2,1,0:T(8,128)(2,1)} %pad_maximum_fusion.fields, f32[256,32,128]{2,1,0:T(8,128)} %bitcast.106, bf16[1024,256]{1,0:T(8,128)(2,1)S(1)} %get-tuple-element.82.first, ...), custom_call_target="tpu_custom_call" | custom-call | flops 9216000000 | bytes 30720000 | tf_op jit(solution)/shard_map/cond/branch_0_fun/student_forward/pallas_call | solution.py:179
  287.1 2.3 reshape.51
  289.4 29.7 %all_to_all.30 = bf16[4,256,1024]{2,1,0:T(8,128)(2,1)S(1)} all-to-all(bf16[4,256,1024]{2,1,0:T(8,128)(2,1)} %get-tuple-element.127), channel_id=1, replica_groups=mesh['grp'=2,'head'=4,'seq'=4] {'seq'}, dimensions={0} | all-to-all | bytes 4194304 | tf_op jit(solution)/shard_map/all_to_all | solution.py:342
  319.1 14.6 %convert_bitcast_fusion = bf16[4096,1024]{0,1:T(8,128)(2,1)} fusion(bf16[1024,1024]{1,0:T(8,128)(2,1)S(1)} %bitcast.112, bf16[1,1024,4096]{2,1,0:T(8,128)(2,1)} %param.20), kind=kOutput, calls=%fused_computation.13 | convolution fusion | flops 8594128896 | bytes 18874368 | tf_op jit(solution)/shard_map/dot_general | solution.py:398
  333.7 44.1 %collective-permute-start.5 = (bf16[3,4096,1024]{2,1,0:T(8,128)(2,1)}, bf16[3,4096,1024]{2,1,0:T(8,128)(2,1)}, u32[]{:S(2)}, u32[]{:S(2)}) collective-permute-start(bf16[3,4096,1024]{2,1,0:T(8,128)(2,1)} %bitcast.114), channel_id=1, source_target_pairs={{16,0},{17,1},{18,2},{19,3},{20,4},{21,5},{22,6},{23,7},{24,8},{25... | collective-permute-start | bytes 75497480 | tf_op jit(solution)/shard_map/ppermute | solution.py:20
  377.8 4.5 collective-permute-start.2
  382.3 68.7 %reduce-scatter.3.cloned.1.call-done = bf16[1024,1024]{0,1:T(8,128)(2,1)} async-done(((bf16[4096,1024]{0,1:T(8,128)(2,1)}), bf16[1024,1024]{0,1:T(8,128)(2,1)}) %reduce-scatter.3.cloned.1.call-update) | async-done | bytes 2097168 | tf_op jit(solution)/shard_map/reduce_scatter | solution.py:397
  453.6 2.3 collective-permute-done.1
  457.6 52.5 %all-gather.5.cloned.1.call-done = bf16[4096,512]{0,1:T(8,128)(2,1)} async-done(((bf16[1024,512]{0,1:T(8,128)(2,1)}), bf16[4096,512]{0,1:T(8,128)(2,1)}) %all-gather.5.cloned.1.call-update) | async-done | bytes 4194320 | tf_op jit(solution)/shard_map/all_gather | solution.py:409
  510.1 9.1 %conditional.13 = (bf16[1024,512]{1,0:T(8,128)(2,1)S(1)}) conditional(s32[]{:T(128)} %convert_element_type.53, (bf16[1024,4096]{1,0:T(8,128)(2,1)}, bf16[4096,512]{0,1:T(8,128)(2,1)}) %tuple.78, (bf16[1024,4096]{1,0:T(8,128)(2,1)}, bf16[4096,512]{0,1:T(8,128)(2,1)}) %tuple.45), branch_computations={%region_3.4_spmd, %region_4.5_spmd} | conditional | flops 4294967296 | bytes 13631496
  510.1 9.1 %fusion.26 = bf16[1024,512]{1,0:T(8,128)(2,1)S(1)} fusion(bf16[1024,4096]{1,0:T(8,128)(2,1)} %get-tuple-element.95, bf16[4096,512]{0,1:T(8,128)(2,1)} %get-tuple-element.144), kind=kOutput, calls=%fused_computation.39 | convolution fusion | flops 4294967296 | bytes 13631488 | tf_op jit(solution)/shard_map/cond/branch_0_fun/dot_general | solution.py:412
  519.3 29.1 %all_to_all.31 = bf16[4,256,512]{2,1,0:T(8,128)(2,1)S(1)} all-to-all(bf16[4,256,512]{2,1,0:T(8,128)(2,1)S(1)} %bitcast.113), channel_id=1, replica_groups=mesh['grp'=2,'head'=4,'seq'=4] {'seq'}, dimensions={0} | all-to-all | bytes 2097152 | tf_op jit(solution)/shard_map/all_to_all | solution.py:342
  549.7 3.9 collective-permute-done.3
  553.9 66.7 %conditional.14 = (bf16[4,3,256,512]{3,2,1,0:T(8,128)(2,1)}, bf16[4,3,256,512]{3,2,1,0:T(8,128)(2,1)}, f32[256,4096]{1,0:T(8,128)}) conditional(s32[]{:T(128)} %convert_element_type.53, (bf16[4,256,1024]{2,1,0:T(8,128)(2,1)}, bf16[4,256,1024]{2,1,0:T(8,128)(2,1)}, bf16[4,256,1024]{2,1,0:T(8,128)(2,1)S(1)}, bf16[4,256,1024]{2,1,0:T(8,128)(2,1)S(1)}, ...), branch_computations={%region_5.6_spmd, %region_6.7_spmd} | conditional | flops 9222291456 | bytes 118800456 | solution.py:440
  556.6 2.2 copy.30
  559.4 3.4 pad_maximum_fusion.1.fields
  565.1 27.0 %student_backward.1 = (bf16[4,3,256,8,128]{4,3,2,1,0:T(8,128)(2,1)}, f32[256,32,128]{2,1,0:T(8,128)}) custom-call(bf16[3,4,256,8,128]{4,3,2,1,0:T(8,128)(2,1)} %pad_maximum_fusion.1.fields, bf16[4,256,8,128]{3,2,1,0:T(8,128)(2,1)S(1)} %bitcast.91, f32[256,32,128]{2,1,0:T(8,128)} %get-tuple-element.103.conv, bf16[16384,256]{1,0:T(8,128)(2,1)S(1)} %bitcast.119, ...), custom_call_target="tpu_custom_call" | custom-call | flops 9216000000 | bytes 30720000 | tf_op jit(solution)/shard_map/cond/branch_0_fun/student_backward/pallas_call | solution.py:206
  592.1 9.0 %fusion.25 = (bf16[4,3,256,4,128]{4,3,2,1,0:T(4,128)(2,1)}, bf16[4,3,256,4,128]{4,3,2,1,0:T(4,128)(2,1)}) fusion(bf16[4,3,256,8,128]{4,3,2,1,0:T(8,128)(2,1)} %get-tuple-element.112), kind=kLoop, calls=%fused_computation.38 | loop fusion | bytes 12582912 | tf_op jit(solution)/shard_map/cond/branch_0_fun/slice | solution.py:434
  601.2 5.7 reshape.54
  606.9 5.7 reshape.55
  612.6 8.1 %copy.37 = f32[32,8,32,128]{3,1,2,0:T(8,128)} copy(f32[32,8,32,128]{3,2,1,0:T(8,128)} %bitcast.105) | data formatting | bytes 8388608 | tf_op jit(solution)/shard_map/cond
  622.1 5.3 collective-permute-done.4
  627.4 2.3 broadcast_select_fusion.2
  629.7 72.4 %all_to_all.32 = bf16[4,3,256,512]{3,2,1,0:T(8,128)(2,1)S(1)} all-to-all(bf16[4,3,256,512]{3,2,1,0:T(8,128)(2,1)S(1)} %broadcast_select_fusion.2), channel_id=1, replica_groups=mesh['grp'=2,'head'=4,'seq'=4] {'seq'}, dimensions={0} | all-to-all | bytes 6291456 | tf_op jit(solution)/shard_map/all_to_all | solution.py:342
  702.3 19.6 %conditional.15 = (bf16[4096,512]{1,0:T(8,128)(2,1)}) conditional(s32[]{:T(128)} %convert_element_type.53, (bf16[3,4096,1024]{2,1,0:T(8,128)(2,1)}, bf16[3,1024,512]{2,1,0:T(8,128)(2,1)S(1)}) %tuple.77, (bf16[3,4096,1024]{2,1,0:T(8,128)(2,1)}, bf16[3,1024,512]{2,1,0:T(8,128)(2,1)S(1)}) %tuple.76), branch_computations={%region_7.8_spmd, %region_8.9_spmd} | conditional | flops 12884901888 | bytes 32505864
  702.5 19.4 %convolution_bitcast_fusion = bf16[4096,512]{1,0:T(8,128)(2,1)} fusion(bf16[3,4096,1024]{2,1,0:T(8,128)(2,1)} %get-tuple-element.114, bf16[3,1024,512]{2,1,0:T(8,128)(2,1)S(1)} %get-tuple-element.115), kind=kOutput, calls=%fused_computation.4 | convolution fusion | flops 12884901888 | bytes 32505856 | tf_op jit(solution)/shard_map/cond/branch_0_fun/dot_general | solution.py:447
  721.9 6.5 copy.22
  730.2 2.6 collective-permute-start.7
  732.8 46.0 %reduce-scatter.5.cloned.1.call-done = bf16[1024,512]{0,1:T(8,128)(2,1)} async-done(((bf16[4096,512]{0,1:T(8,128)(2,1)}), bf16[1024,512]{0,1:T(8,128)(2,1)}) %reduce-scatter.5.cloned.1.call-update) | async-done | bytes 1048592 | tf_op jit(solution)/shard_map/reduce_scatter | solution.py:459
  780.2 3.5 slice_select_fusion
  783.7 2.3 fusion.11
  (56 shorter events, 20.5 us)
Async XLA Ops:
  7.2 58.1 %all-gather.3.cloned.1.call-start = ((), (), s32[]{:S(2)}) async-start(), calls=%async_computation.8 | async-start | bytes 5242880 | tf_op jit(solution)/shard_map/all_gather | solution.py:362
  65.2 7.7 collective-permute-start
  93.2 52.1 %all-to-all-start.2 = ((bf16[4,256,1024]{2,1,0:T(8,128)(2,1)}), bf16[4,256,1024]{2,1,0:T(8,128)(2,1)S(1)}, u32[]{:S(2)}, u32[]{:S(2)}) async-start(bf16[4,256,1024]{2,1,0:T(8,128)(2,1)} %bitcast.111), calls=%async_computation.2 | async-start | bytes 4194304 | tf_op jit(solution)/shard_map/all_to_all | solution.py:342
  145.3 104.9 %copy-start.1 = (bf16[4,256,1024]{2,1,0:T(8,128)(2,1)}, bf16[4,256,1024]{2,1,0:T(8,128)(2,1)S(1)}, u32[]{:S(2)}) copy-start(bf16[4,256,1024]{2,1,0:T(8,128)(2,1)S(1)} %all-to-all-done.2) | copy-start | bytes 6291460
  145.3 52.7 %all-to-all-start.1 = ((bf16[4,256,1024]{2,1,0:T(8,128)(2,1)}), bf16[4,256,1024]{2,1,0:T(8,128)(2,1)}, u32[]{:S(2)}, u32[]{:S(2)}) async-start(bf16[4,256,1024]{2,1,0:T(8,128)(2,1)} %bitcast.110), calls=%async_computation.1 | async-start | bytes 4194304 | tf_op jit(solution)/shard_map/all_to_all | solution.py:342
  165.3 84.9 %copy-start.5 = (bf16[1024,256]{1,0:T(8,128)(2,1)S(1)}, bf16[1024,256]{1,0:T(8,128)(2,1)}, u32[]{:S(2)}) copy-start(bf16[1024,256]{1,0:T(8,128)(2,1)} %constant.28.clone) | copy-start | bytes 1572868
  165.3 84.9 %copy-start.7 = (bf16[256,256]{1,0:T(8,128)(2,1)S(1)}, bf16[256,256]{1,0:T(8,128)(2,1)}, u32[]{:S(2)}) copy-start(bf16[256,256]{1,0:T(8,128)(2,1)} %constant.29.clone) | copy-start | bytes 393220
  165.3 84.9 %copy-start.8 = (bf16[256,256]{1,0:T(8,128)(2,1)S(1)}, bf16[256,256]{1,0:T(8,128)(2,1)}, u32[]{:S(2)}) copy-start(bf16[256,256]{1,0:T(8,128)(2,1)} %constant.30.clone) | copy-start | bytes 393220
  165.3 84.9 %copy-start.9 = (bf16[64,256]{1,0:T(8,128)(2,1)S(1)}, bf16[64,256]{1,0:T(8,128)(2,1)}, u32[]{:S(2)}) copy-start(bf16[64,256]{1,0:T(8,128)(2,1)} %constant.31.clone) | copy-start | bytes 98308
  165.3 84.9 %copy-start.10 = (f32[64,128]{1,0:T(8,128)S(1)}, f32[64,128]{1,0:T(8,128)}, u32[]{:S(2)}) copy-start(f32[64,128]{1,0:T(8,128)} %constant.32.clone) | copy-start | bytes 98308
  165.3 84.9 %copy-start.11 = (f32[64,128]{1,0:T(8,128)S(1)}, f32[64,128]{1,0:T(8,128)}, u32[]{:S(2)}) copy-start(f32[64,128]{1,0:T(8,128)} %constant.33.clone) | copy-start | bytes 98308
  198.0 52.2 %all-to-all-start = ((bf16[4,256,1024]{2,1,0:T(8,128)(2,1)}), bf16[4,256,1024]{2,1,0:T(8,128)(2,1)}, u32[]{:S(2)}, u32[]{:S(2)}) async-start(bf16[4,256,1024]{2,1,0:T(8,128)(2,1)} %bitcast.109), calls=%async_computation | async-start | bytes 4194304 | tf_op jit(solution)/shard_map/all_to_all | solution.py:342
  202.4 248.6 %reduce-scatter.3.cloned.1.call-start = ((), (), s32[]{:S(2)}) async-start(), calls=%async_computation.9 | async-start | bytes 10485760 | tf_op jit(solution)/shard_map/reduce_scatter | solution.py:397
  255.3 4.4 copy-start.3
  333.7 176.4 %all-gather.5.cloned.1.call-start = ((), (), s32[]{:S(2)}) async-start(), calls=%async_computation.10 | async-start | bytes 5242880 | tf_op jit(solution)/shard_map/all_gather | solution.py:409
  333.7 368.6 %collective-permute-start.5 = (bf16[3,4096,1024]{2,1,0:T(8,128)(2,1)}, bf16[3,4096,1024]{2,1,0:T(8,128)(2,1)}, u32[]{:S(2)}, u32[]{:S(2)}) collective-permute-start(bf16[3,4096,1024]{2,1,0:T(8,128)(2,1)} %bitcast.114), channel_id=1, source_target_pairs={{16,0},{17,1},{18,2},{19,3},{20,4},{21,5},{22,6},{23,7},{24,8},{25... | collective-permute-start | bytes 75497480 | tf_op jit(solution)/shard_map/ppermute | solution.py:20
  377.8 132.3 %collective-permute-start.2 = (bf16[1024,4096]{1,0:T(8,128)(2,1)}, bf16[1024,4096]{1,0:T(8,128)(2,1)}, u32[]{:S(2)}, u32[]{:S(2)}) collective-permute-start(bf16[1024,4096]{1,0:T(8,128)(2,1)} %bitcast.116), channel_id=1, source_target_pairs={{16,0},{17,1},{18,2},{19,3},{20,4},{21,5},{22,6},{23,7},{24,8},{25... | collective-permute-start | bytes 25165832 | tf_op jit(solution)/shard_map/ppermute | solution.py:20
  451.0 4.9 copy-start
  452.8 3.1 collective-permute-start.1
  457.6 321.2 %reduce-scatter.5.cloned.1.call-start = ((), (), s32[]{:S(2)}) async-start(), calls=%async_computation.11 | async-start | bytes 5242880 | tf_op jit(solution)/shard_map/reduce_scatter | solution.py:459
  519.2 34.7 %copy-start.2 = (bf16[4,256,1024]{2,1,0:T(8,128)(2,1)S(1)}, bf16[4,256,1024]{2,1,0:T(8,128)(2,1)}, u32[]{:S(2)}) copy-start(bf16[4,256,1024]{2,1,0:T(8,128)(2,1)} %copy-done.1) | copy-start | bytes 6291460
  519.2 34.7 %copy-start.6 = (bf16[1024,256]{1,0:T(8,128)(2,1)S(1)}, bf16[1024,256]{1,0:T(8,128)(2,1)}, u32[]{:S(2)}) copy-start(bf16[1024,256]{1,0:T(8,128)(2,1)} %constant.28.clone) | copy-start | bytes 1572868
  548.4 5.2 collective-permute-start.3
  559.4 4.4 slice-start
  559.4 5.7 slice-start.1
  620.7 6.8 collective-permute-start.4
  730.2 50.0 %collective-permute-start.7 = (bf16[256,2048]{1,0:T(8,128)(2,1)S(1)}, bf16[256,2048]{1,0:T(8,128)(2,1)}, u32[]{:S(2)}, u32[]{:S(2)}) collective-permute-start(bf16[256,2048]{1,0:T(8,128)(2,1)S(1)} %slice.75), channel_id=1, source_target_pairs={{16,0},{17,1},{18,2},{19,3},{20,4},{21,5},{22,6},{23,7},{24,8},{25... | collective-permute-start | bytes 3145736 | tf_op jit(solution)/shard_map/ppermute | solution.py:20
  778.7 5.0 copy-start.4
  778.7 5.0 collective-permute-start.6
Sparse Core Ops, SparseCore 0:
  10.4 54.7 all-gather.2
  333.8 117.1 reduce-scatter.2
  457.7 52.3 all-gather.4
  728.5 50.1 reduce-scatter.4
